TPU v7x, 32 devices: a whole 2x2x4 slice. The times are simulated.
32 devices in a mesh: leaf: 8 (over z, y), chan: 4 (over x, core).
Axes of the slice: x: 2, y: 2, z: 4, core: 2. Of those that a mesh axis runs over, the one named last changes fastest.
Arguments:
- features: bfloat16 [64, 32768], P(None, 'leaf'), may hold values from -6 to 6
- neighbours: int32 [27, 32768], P(None, 'leaf'), may hold values from -1 to 2048, as said below
- child_count: int32 [8], P('leaf'), may hold values from 1024 to 4096, as said below
- dest: int32 [4096], P('leaf'), may hold values from -1 to 4095, as said below
- conv_weight: bfloat16 [27, 64, 64], P(None, None, 'chan'), may hold values from -0.15625 to 0.15625
- merge_weight: bfloat16 [8, 64, 128], P(None, None, 'chan'), may hold values from -0.25 to 0.25
- parent_grad: bfloat16 [128, 4096], P('chan', 'leaf'), may hold values from -6 to 6
Outputs:
- parents: bfloat16 [128, 4096], P('chan', 'leaf')
- merge_weight_grad: float32 [8, 64, 128], P(None, None, 'chan')
Inputs may be any that keep to these rules, and one draw needn't show every extreme that they name: `neighbours`: entry [k, r] is -1 where the neighbour is empty; else r + entry - 1024 is the index of a valid child octant, so the entry lies in 0 to 2048. Slots beyond a device's valid octants may hold entries too. Row 13 holds 1024 for every valid r. `child_count`: A multiple of 8; the valid child octants are the first ones of each device's 4096 slots; in every draw some device is full. `dest`: for parent slot g of device d, valid where g < child_count[d] / 8: t // 512 is the owner device and t % 512 = d * 64 + g % 64; the 64 slots with one value of g // 64 share an owner, and distinct such blocks of one device have distinct owners; -1 where g is not valid.
All inputs are finite; a program needn't handle non-finite values.
Results may differ from a plain program's by a relative error of at most 0.005.
Values may be sent and summed in bfloat16 or wider, within the bound.
A program may use at most 64 MiB of HBM per device.

v0:
```python
import math

import jax
import jax.numpy as jnp
from jax import lax
from jax.sharding import PartitionSpec as P

KIDS = 8
PG = 512
HALO = 1024


def passed_along(value, axis, steps):
    count = lax.axis_size(axis)
    initial, last = (max(0, -steps), min(count, count - steps))
    return lax.ppermute(value, axis, [(source, source + steps) for source in range(initial, last)])


def tap_conv(window, offsets, weight, first_global, valid_rows, pieces):
    row_total = offsets.shape[1]
    block_rows = row_total // pieces
    out_width = weight.shape[2]

    def conv_block(first_row):
        offset_block = lax.dynamic_slice_in_dim(offsets, first_row, block_rows, 1)
        present = offset_block >= 0
        local_rows = first_row + jnp.arange(block_rows, dtype=jnp.int32)
        local_index = jnp.where(present, local_rows[None, :] + offset_block, 0)
        gathered = window[:, local_index] * present.astype(jnp.bfloat16)[None]
        pre_act = jnp.einsum("ckr,kco->or", gathered, weight, preferred_element_type=jnp.float32)
        living = first_global + local_rows < valid_rows
        return (jnp.maximum(pre_act, 0.0) * living[None, :]).astype(jnp.bfloat16)

    stacked = lax.map(conv_block, jnp.arange(pieces, dtype=jnp.int32) * block_rows)
    return jnp.moveaxis(stacked, 0, 1).reshape(out_width, row_total)


def per_device(features, neighbours, child_count, dest, conv_weight, merge_weight, parent_grad):
    row_count = features.shape[1]
    in_width = features.shape[0]
    out_merge = merge_weight.shape[2]
    group_count = row_count // KIDS
    peer_count = lax.axis_size("leaf")
    pair_slots = group_count // peer_count
    valid_rows = child_count[0]
    quarter = row_count // lax.axis_size("chan")
    first_global = lax.axis_index("chan") * quarter
    before = passed_along(features[:, row_count - HALO :], "leaf", 1)
    after = passed_along(features[:, :HALO], "leaf", -1)
    extended = jnp.concatenate([before, features, after], axis=1)
    window = lax.dynamic_slice_in_dim(extended, first_global, quarter + 2 * HALO, 1)
    offsets = lax.dynamic_slice_in_dim(neighbours, first_global, quarter, 1)
    conv_all = lax.all_gather(conv_weight, "chan", axis=2, tiled=True)
    hidden_rows = tap_conv(window, offsets, conv_all, first_global, valid_rows, 4)
    grouped_rows = hidden_rows.reshape(in_width, quarter // KIDS, KIDS)
    merge_all = lax.all_gather(merge_weight, "chan", axis=2, tiled=True)
    merged_rows = jnp.einsum(
        "cqk,kco->oq", grouped_rows, merge_all, preferred_element_type=jnp.float32
    ).astype(jnp.bfloat16)
    merged = lax.all_to_all(merged_rows, "chan", split_axis=0, concat_axis=1, tiled=True)
    living_group = dest >= 0
    owner_dev = jnp.where(living_group, dest // group_count, 0)
    within = dest % pair_slots
    target_owner = jnp.where(living_group, owner_dev, peer_count)
    outbox = jnp.zeros((out_merge, peer_count, pair_slots), jnp.bfloat16)
    outbox = outbox.at[:, target_owner, within].set(merged, mode="drop")
    arrived = lax.all_to_all(outbox, "leaf", split_axis=1, concat_axis=1, tiled=True)
    parents = arrived.reshape(out_merge, group_count)
    returned = lax.all_to_all(
        parent_grad.reshape(out_merge, peer_count, pair_slots),
        "leaf",
        split_axis=1,
        concat_axis=1,
        tiled=True,
    )
    fetched = returned[:, owner_dev, within] * living_group.astype(jnp.bfloat16)[None, :]
    fetched_rows = lax.all_to_all(fetched, "chan", split_axis=1, concat_axis=0, tiled=True)
    weight_full = jnp.einsum(
        "cqk,oq->kco", grouped_rows, fetched_rows, preferred_element_type=jnp.float32
    )
    weight_term = lax.psum_scatter(weight_full, "chan", scatter_dimension=2, tiled=True)
    merge_weight_grad = lax.psum(weight_term, "leaf") / math.sqrt(KIDS * PG)
    return (parents, merge_weight_grad)


def solution(mesh):
    in_specs = (
        P(None, "leaf"),
        P(None, "leaf"),
        P("leaf"),
        P("leaf"),
        P(None, None, "chan"),
        P(None, None, "chan"),
        P("chan", "leaf"),
    )
    out_specs = (P("chan", "leaf"), P(None, None, "chan"))
    return jax.shard_map(
        per_device, mesh=mesh, in_specs=in_specs, out_specs=out_specs, check_vma=False
    )
```

profile of v0, /device:TPU:0, one launch (start us, length us, event | category | flops | bytes accessed | tf_op | source)
XLA Modules:
  0.0 231.5 jit_solution(6221487790897557289)
XLA Ops:
  7.2 1.6 copy.44
  8.8 4.9 %collective-permute-start = (bf16[64,1024]{0,1:T(8,128)(2,1)S(1)}, bf16[64,1024]{0,1:T(8,128)(2,1)S(1)}, u32[]{:S(2)}, u32[]{:S(2)}) collective-permute-start(bf16[64,1024]{0,1:T(8,128)(2,1)S(1)} %get-tuple-element.72), channel_id=1, source_target_pairs={{0,4},{4,8},{8,12},{12,16},{16,20},{20,24},{24,28},{1,5},{5,9},{9,... | collective-permute-start | bytes 393224 | tf_op jit(solution)/shard_map/ppermute | solution.py:16
  15.9 7.0 %all-to-all-start.2 = ((bf16[8,2,1024]{2,1,0:T(2,128)(2,1)}), bf16[8,2,1024]{2,1,0:T(2,128)(2,1)S(1)}, u32[]{:S(2)}, u32[]{:S(2)}) async-start(bf16[8,2,1024]{2,1,0:T(2,128)(2,1)} %reshape.70), calls=%async_computation.2 | async-start | bytes 65536 | tf_op jit(solution)/shard_map/all_to_all | solution.py:69
  23.0 7.2 %all_gather.6 = bf16[27,64,64]{1,2,0:T(8,128)(2,1)} all-gather(bf16[27,64,16]{1,2,0:T(8,128)(2,1)S(1)} %copy-done.1), channel_id=1, replica_groups=mesh['leaf'=8,'chan'=4] {'chan'}, dimensions={2}, use_global_device_ids=true | all-gather | bytes 276480 | tf_op jit(solution)/shard_map/all_gather | solution.py:53
  30.4 3.2 %gather_fusion.1 = bf16[512,32]{1,0:T(8,128)(2,1)S(1)} fusion(bf16[32,8,64]{0,2,1:T(8,128)(2,1)S(1)} %copy.53, s32[512]{0:T(512)S(1)} %bitcast.79), kind=kCustom, calls=%fused_computation.1 | custom fusion | bytes 69632 | tf_op jit(solution)/shard_map/gather | solution.py:76
  34.3 3.3 %all-to-all-start.3 = ((bf16[32,4,128]{2,0,1:T(8,128)(2,1)}), bf16[32,4,128]{2,0,1:T(8,128)(2,1)S(1)}, u32[]{:S(2)}, u32[]{:S(2)}) async-start(bf16[32,4,128]{2,0,1:T(8,128)(2,1)} %broadcast_multiply_fusion.1), calls=%async_computation.3 | async-start | bytes 65536 | tf_op jit(solution)/shard_map/all_to_all | solution.py:77
  37.7 2.9 %fusion.10 = bf16[64,3072]{0,1:T(8,128)(2,1)S(1)} fusion(s32[]{:T(128)S(6)} %select_n.52, bf16[64,1024]{0,1:T(8,128)(2,1)S(1)} %collective-permute-done, bf16[64,4096]{0,1:T(8,128)(2,1)S(1)} %copy.44, bf16[64,1024]{0,1:T(8,128)(2,1)S(1)} %collective-permute-done.1), kind=kLoop, calls=%fused_computation.24 | loop fusion | flops 1179648 | bytes 1179652 | tf_op jit(solution)/shard_map/concatenate | solution.py:50
  40.6 83.7 %while.10 = (s32[]{:T(128)}, bf16[4,64,256]{2,1,0:T(8,128)(2,1)S(1)}, s32[4]{0:T(128)S(1)}, s32[27,1024]{1,0:T(8,128)S(1)}, bf16[64,3072]{0,1:T(8,128)(2,1)S(1)}...) while((s32[]{:T(128)}, ...), condition=%wide.region_1.2_spmd, body=%wide.region_0.1_spmd.sunk | while | flops 57171460 | bytes 4948151 | solution.py:34
  44.0 13.1 %gather_fusion = bf16[6912,64]{1,0:T(8,128)(2,1)S(1)} fusion(bf16[64,3072]{0,1:T(8,128)(2,1)S(1)} %get-tuple-element.157, s32[7168]{0:T(1024)S(1)} %pad_clamp_fusion.2), kind=kCustom, calls=%fused_computation.clone.1 | custom fusion | bytes 1797120 | tf_op jit(solution)/shard_map/while/body/eval_jaxpr/gather | solution.py:29
  57.0 1.5 copy.61
  59.9 1.6 fusion.32
  64.9 13.1 %gather_fusion = bf16[6912,64]{1,0:T(8,128)(2,1)S(1)} fusion(bf16[64,3072]{0,1:T(8,128)(2,1)S(1)} %get-tuple-element.157, s32[7168]{0:T(1024)S(1)} %pad_clamp_fusion.2), kind=kCustom, calls=%fused_computation.clone.1 | custom fusion | bytes 1797120 | tf_op jit(solution)/shard_map/while/body/eval_jaxpr/gather | solution.py:29
  78.0 1.5 copy.61
  80.8 1.6 fusion.32
  85.8 13.1 %gather_fusion = bf16[6912,64]{1,0:T(8,128)(2,1)S(1)} fusion(bf16[64,3072]{0,1:T(8,128)(2,1)S(1)} %get-tuple-element.157, s32[7168]{0:T(1024)S(1)} %pad_clamp_fusion.2), kind=kCustom, calls=%fused_computation.clone.1 | custom fusion | bytes 1797120 | tf_op jit(solution)/shard_map/while/body/eval_jaxpr/gather | solution.py:29
  101.7 1.6 fusion.32
  106.8 13.1 %gather_fusion = bf16[6912,64]{1,0:T(8,128)(2,1)S(1)} fusion(bf16[64,3072]{0,1:T(8,128)(2,1)S(1)} %get-tuple-element.157, s32[7168]{0:T(1024)S(1)} %pad_clamp_fusion.2), kind=kCustom, calls=%fused_computation.clone.1 | custom fusion | bytes 1797120 | tf_op jit(solution)/shard_map/while/body/eval_jaxpr/gather | solution.py:29
  122.7 1.6 fusion.32
  125.9 6.2 %all_gather.7 = bf16[8,64,128]{1,2,0:T(8,128)(2,1)S(1)} all-gather(bf16[8,64,32]{1,2,0:T(8,128)(2,1)S(1)} %copy-done.2), channel_id=1, replica_groups=mesh['leaf'=8,'chan'=4] {'chan'}, dimensions={2}, use_global_device_ids=true | all-gather | bytes 163840 | tf_op jit(solution)/shard_map/all_gather | solution.py:56
  133.0 3.3 %all-to-all-start = ((bf16[4,32,128]{2,1,0:T(8,128)(2,1)}), bf16[4,32,128]{2,1,0:T(8,128)(2,1)S(1)}, u32[]{:S(2)}, u32[]{:S(2)}) async-start(bf16[4,32,128]{2,1,0:T(8,128)(2,1)} %bitcast.14), calls=%async_computation | async-start | bytes 65536 | tf_op jit(solution)/shard_map/all_to_all | solution.py:60
  136.3 13.3 %reduce-scatter.2.cloned.1.call-done = f32[8,64,32]{1,0,2:T(8,128)} async-done(((f32[8,64,128]{1,0,2:T(8,128)}), f32[8,64,32]{1,0,2:T(8,128)}) %reduce-scatter.2.cloned.1.call-update) | async-done | bytes 65552 | tf_op jit(solution)/shard_map/reduce_scatter | solution.py:81
  149.8 26.0 %scatter_fusion = bf16[32,8,64]{0,2,1:T(8,128)(2,1)S(1)} fusion(bf16[32,8,64]{0,2,1:T(8,128)(2,1)S(1)} %broadcast_in_dim.34, s32[512]{0:T(512)S(1)} %bitcast.78, bf16[512,32]{1,0:T(8,128)(2,1)S(1)} %bitcast.85), kind=kCustom, calls=%fused_computation.2 | custom fusion | bytes 102400 | tf_op jit(solution)/shard_map/scatter | solution.py:66
  176.1 12.2 %all_to_all.45 = bf16[8,2,1024]{2,1,0:T(2,128)(2,1)S(1)} all-to-all(bf16[8,2,1024]{2,1,0:T(2,128)(2,1)S(1)} %reshape.68), channel_id=1, replica_groups=mesh['leaf'=8,'chan'=4] {'leaf'}, dimensions={0} | all-to-all | bytes 65536 | tf_op jit(solution)/shard_map/all_to_all | solution.py:67
  189.1 33.9 %all-reduce.2.cloned.1.call-done = f32[8,64,32]{1,0,2:T(8,128)} async-done(((f32[8,64,32]{1,0,2:T(8,128)}), f32[8,64,32]{1,0,2:T(8,128)}) %all-reduce.2.cloned.1.call-update) | async-done | bytes 65552 | tf_op jit(solution)/shard_map/psum | solution.py:82
  (78 shorter events, 22.7 us)
Async XLA Ops:
  7.2 15.7 %copy-start = (s32[27,4096]{1,0:T(8,128)S(1)}, s32[27,4096]{1,0:T(8,128)}, u32[]{:S(2)}) copy-start(s32[27,4096]{1,0:T(8,128)} %param.10) | copy-start | bytes 1327108
  7.2 7.9 %copy-start.3 = (bf16[32,512]{1,0:T(8,128)(2,1)S(1)}, bf16[32,512]{1,0:T(8,128)(2,1)}, u32[]{:S(2)}) copy-start(bf16[32,512]{1,0:T(8,128)(2,1)} %param.15) | copy-start | bytes 98308
  7.2 15.7 %copy-start.4 = (s32[512]{0:T(512)S(1)}, s32[512]{0:T(512)}, u32[]{:S(2)}) copy-start(s32[512]{0:T(512)} %param.12) | copy-start | bytes 6148
  7.2 15.8 %copy-start.1 = (bf16[27,64,16]{1,2,0:T(8,128)(2,1)S(1)}, bf16[27,64,16]{1,2,0:T(8,128)(2,1)}, u32[]{:S(2)}) copy-start(bf16[27,64,16]{1,2,0:T(8,128)(2,1)} %param.13) | copy-start | bytes 165892
  8.8 28.8 %collective-permute-start = (bf16[64,1024]{0,1:T(8,128)(2,1)S(1)}, bf16[64,1024]{0,1:T(8,128)(2,1)S(1)}, u32[]{:S(2)}, u32[]{:S(2)}) collective-permute-start(bf16[64,1024]{0,1:T(8,128)(2,1)S(1)} %get-tuple-element.72), channel_id=1, source_target_pairs={{0,4},{4,8},{8,12},{12,16},{16,20},{20,24},{24,28},{1,5},{5,9},{9,... | collective-permute-start | bytes 393224 | tf_op jit(solution)/shard_map/ppermute | solution.py:16
  13.7 23.9 %collective-permute-start.1 = (bf16[64,1024]{0,1:T(8,128)(2,1)S(1)}, bf16[64,1024]{0,1:T(8,128)(2,1)S(1)}, u32[]{:S(2)}, u32[]{:S(2)}) collective-permute-start(bf16[64,1024]{0,1:T(8,128)(2,1)S(1)} %get-tuple-element.71), channel_id=1, source_target_pairs={{4,0},{8,4},{12,8},{16,12},{20,16},{24,20},{28,24},{5,1},{9,5},{13... | collective-permute-start | bytes 393224 | tf_op jit(solution)/shard_map/ppermute | solution.py:16
  15.9 14.3 %all-to-all-start.2 = ((bf16[8,2,1024]{2,1,0:T(2,128)(2,1)}), bf16[8,2,1024]{2,1,0:T(2,128)(2,1)S(1)}, u32[]{:S(2)}, u32[]{:S(2)}) async-start(bf16[8,2,1024]{2,1,0:T(2,128)(2,1)} %reshape.70), calls=%async_computation.2 | async-start | bytes 65536 | tf_op jit(solution)/shard_map/all_to_all | solution.py:69
  34.3 90.4 %all-to-all-start.3 = ((bf16[32,4,128]{2,0,1:T(8,128)(2,1)}), bf16[32,4,128]{2,0,1:T(8,128)(2,1)S(1)}, u32[]{:S(2)}, u32[]{:S(2)}) async-start(bf16[32,4,128]{2,0,1:T(8,128)(2,1)} %broadcast_multiply_fusion.1), calls=%async_computation.3 | async-start | bytes 65536 | tf_op jit(solution)/shard_map/all_to_all | solution.py:77
  37.6 112.0 %reduce-scatter.2.cloned.1.call-start = ((), (), s32[]{:S(2)}) async-start(), calls=%async_computation.5 | async-start | bytes 655360 | tf_op jit(solution)/shard_map/reduce_scatter | solution.py:81
  124.3 1.6 copy-start.2
  133.0 16.7 %all-to-all-start = ((bf16[4,32,128]{2,1,0:T(8,128)(2,1)}), bf16[4,32,128]{2,1,0:T(8,128)(2,1)S(1)}, u32[]{:S(2)}, u32[]{:S(2)}) async-start(bf16[4,32,128]{2,1,0:T(8,128)(2,1)} %bitcast.14), calls=%async_computation | async-start | bytes 65536 | tf_op jit(solution)/shard_map/all_to_all | solution.py:60
  136.2 86.8 %all-reduce.2.cloned.1.call-start = ((), (), s32[]{:S(2)}) async-start(), calls=%async_computation.6 | async-start | bytes 262144 | tf_op jit(solution)/shard_map/psum | solution.py:82
Sparse Core Ops, SparseCore 0:
  126.0 23.5 reduce-scatter.1
  153.3 69.6 all-reduce.1
where the time goes:
time: 232 us; the launch traced here: 231 us
  local copies, waits for them, and re-layouts  96.3 us (42%)
  waiting for transfers between devices  47.3 us (20%)
  blocking collectives  25.5 us (11%)
  starting transfers between devices  19.7 us (8%)
  between operations  14.3 us (6%)
  other arithmetic  12.8 us (6%)
  loops' own time  7.89 us (3%)
  matrix products  7.5 us (3%)
    gather x8, local copies, waits for them, and re-layouts, conv_block(): gathered = window[:, local_index] * present.astype(jnp.bfloat16)[None]  58.3 us
    psum x1, waiting for transfers between devices, per_device(): merge_weight_grad = lax.psum(weight_term, 'leaf') / math.sqrt(KIDS * PG)  33.9 us
    scatter x2, local copies, waits for them, and re-layouts, per_device(): outbox = outbox.at[:, target_owner, within].set(merged, mode='drop')  26.2 us
    reduce_scatter x1, waiting for transfers between devices, per_device(): lax.psum_scatter(weight_full, 'chan', scatter_dimension=2, tiled=True)  13.3 us
    all_to_all x1, blocking collectives, per_device(): lax.all_to_all(outbox, 'leaf', split_axis=1, concat_axis=1, tiled=True)  12.2 us
    another operation x1, loops' own time, tap_conv(): lax.map(conv_block, jnp.arange(pieces, dtype=jnp.int32) * block_rows)  7.89 us
    all_gather x1, blocking collectives, per_device(): conv_all = lax.all_gather(conv_weight, 'chan', axis=2, tiled=True)  7.19 us
    all_to_all x1, starting transfers between devices, per_device(): lax.all_to_all(parent_grad.reshape(out_merge, peer_count, pair_slots), 'l...  6.96 us
  transfers between devices with their start and end apart: 7, of which 2 were waited for; matrix products, arithmetic and copies ran while one was open for 48% of the time, Pallas kernels for 0%

commit v1 on v0

v1 whole, which is shorter than its diff:
```python
import math

import jax
import jax.numpy as jnp
from jax import lax
from jax.experimental import pallas as pl
from jax.experimental.pallas import tpu as pltpu
from jax.sharding import PartitionSpec as P

KIDS = 8
HALO = 1024
LO = 256
BLOCK = 256
REACH = (2 * HALO + BLOCK) // LO


def subtree_kernel(window, offsets, alive, conv, merge, fetched, merged, grad, picked, hidden, stacked):
    taps, rows = offsets.shape
    width = conv.shape[0]
    groups = rows // KIDS
    slot = lax.broadcasted_iota(jnp.int32, (LO, BLOCK), 0).astype(jnp.float32).astype(jnp.bfloat16)
    local = lax.broadcasted_iota(jnp.int32, (1, BLOCK), 1)
    for block in range(rows // BLOCK):
        span = pl.ds(block * BLOCK, BLOCK)
        source = window[pl.ds(block * width, REACH * width), :]
        for tap in range(taps):
            offset = offsets[pl.ds(tap, 1), span]
            place = local + offset
            chunk = place // LO
            inner = jnp.where(offset >= 0, place - chunk * LO, -1)
            inner = inner.astype(jnp.float32).astype(jnp.bfloat16)
            hot = jnp.where(slot == inner, jnp.bfloat16(1), jnp.bfloat16(0))
            found = jnp.dot(source, hot, preferred_element_type=jnp.float32)
            taken = found[:width]
            for high in range(1, REACH):
                taken = jnp.where(chunk == high, found[high * width : (high + 1) * width], taken)
            picked[pl.ds(tap * width, width), :] = taken.astype(jnp.bfloat16)
        pre_act = jnp.dot(conv[...], picked[...], preferred_element_type=jnp.float32)
        kept = jnp.maximum(pre_act, 0.0) * alive[:, span]
        hidden[:, span] = kept.astype(jnp.bfloat16)
    source_row = lax.broadcasted_iota(jnp.int32, (rows, groups), 0)
    group_row = lax.broadcasted_iota(jnp.int32, (rows, groups), 1) * KIDS
    for kid in range(KIDS):
        order = jnp.where(source_row == group_row + kid, 1.0, 0.0).astype(jnp.bfloat16)
        sorted_kid = jnp.dot(hidden[...], order, preferred_element_type=jnp.float32)
        stacked[pl.ds(kid * width, width), :] = sorted_kid.astype(jnp.bfloat16)
    merged[...] = jnp.dot(merge[...], stacked[...], preferred_element_type=jnp.float32).astype(
        jnp.bfloat16
    )
    grad[...] = lax.dot_general(
        stacked[...], fetched[...], (((1,), (1,)), ((), ())), preferred_element_type=jnp.float32
    )


def passed_along(value, axis, steps):
    count = lax.axis_size(axis)
    initial, last = (max(0, -steps), min(count, count - steps))
    return lax.ppermute(value, axis, [(source, source + steps) for source in range(initial, last)])


def per_device(features, neighbours, child_count, dest, conv_weight, merge_weight, parent_grad):
    row_count = features.shape[1]
    in_width = features.shape[0]
    taps = neighbours.shape[0]
    out_merge = merge_weight.shape[2]
    group_count = row_count // KIDS
    peer_count = lax.axis_size("leaf")
    chan_count = lax.axis_size("chan")
    pair_slots = group_count // peer_count
    valid_rows = child_count[0]
    quarter = row_count // chan_count
    first_global = lax.axis_index("chan") * quarter
    before = passed_along(features[:, row_count - HALO :], "leaf", 1)
    after = passed_along(features[:, :HALO], "leaf", -1)
    extended = jnp.concatenate([before, features, after], axis=1)
    window = lax.dynamic_slice_in_dim(extended, first_global, quarter + 2 * HALO, 1)
    window = window.reshape(in_width, -1, LO).swapaxes(0, 1).reshape(-1, LO)
    offsets = lax.dynamic_slice_in_dim(neighbours, first_global, quarter, 1)
    conv_all = lax.all_gather(conv_weight, "chan", axis=2, tiled=True)
    merge_all = lax.all_gather(merge_weight, "chan", axis=2, tiled=True)
    conv_rows = conv_all.reshape(taps * in_width, in_width).T
    merge_rows = merge_all.reshape(KIDS * in_width, -1).T
    living_rows = first_global + jnp.arange(quarter, dtype=jnp.int32)[None, :] < valid_rows
    alive = living_rows.astype(jnp.float32)

    living_group = dest >= 0
    owner_dev = jnp.where(living_group, dest // group_count, 0)
    within = dest % pair_slots
    target_owner = jnp.where(living_group, owner_dev, peer_count)
    returned = lax.all_to_all(
        parent_grad.reshape(out_merge, peer_count, pair_slots),
        "leaf",
        split_axis=1,
        concat_axis=1,
        tiled=True,
    )
    fetched = returned[:, owner_dev, within] * living_group.astype(jnp.bfloat16)[None, :]
    fetched_rows = lax.all_to_all(fetched, "chan", split_axis=1, concat_axis=0, tiled=True)

    whole = pl.BlockSpec(memory_space=pltpu.VMEM)
    all_merge = out_merge * chan_count
    merged_rows, weight_full = pl.pallas_call(
        subtree_kernel,
        out_shape=(
            jax.ShapeDtypeStruct((all_merge, quarter // KIDS), jnp.bfloat16),
            jax.ShapeDtypeStruct((KIDS * in_width, all_merge), jnp.float32),
        ),
        in_specs=[whole] * 6,
        out_specs=(whole, whole),
        scratch_shapes=[
            pltpu.VMEM((taps * in_width, BLOCK), jnp.bfloat16),
            pltpu.VMEM((in_width, quarter), jnp.bfloat16),
            pltpu.VMEM((KIDS * in_width, quarter // KIDS), jnp.bfloat16),
        ],
        compiler_params=pltpu.CompilerParams(vmem_limit_bytes=40 * 1024 * 1024),
    )(window, offsets, alive, conv_rows, merge_rows, fetched_rows)

    merged = lax.all_to_all(merged_rows, "chan", split_axis=0, concat_axis=1, tiled=True)
    outbox = jnp.zeros((out_merge, peer_count, pair_slots), jnp.bfloat16)
    outbox = outbox.at[:, target_owner, within].set(merged, mode="drop")
    arrived = lax.all_to_all(outbox, "leaf", split_axis=1, concat_axis=1, tiled=True)
    parents = arrived.reshape(out_merge, group_count)
    weight_full = weight_full.reshape(KIDS, in_width, all_merge)
    weight_term = lax.psum_scatter(weight_full, "chan", scatter_dimension=2, tiled=True)
    merge_weight_grad = lax.psum(weight_term, "leaf") / math.sqrt(KIDS * group_count)
    return (parents, merge_weight_grad)


def solution(mesh):
    in_specs = (
        P(None, "leaf"),
        P(None, "leaf"),
        P("leaf"),
        P("leaf"),
        P(None, None, "chan"),
        P(None, None, "chan"),
        P("chan", "leaf"),
    )
    out_specs = (P("chan", "leaf"), P(None, None, "chan"))
    return jax.shard_map(
        per_device, mesh=mesh, in_specs=in_specs, out_specs=out_specs, check_vma=False
    )
```

time: 232 us -> 166 us (0.72)
  local copies, waits for them, and re-layouts: 96.3 us -> 35.5 us
  Pallas kernels: 0 us -> 11.2 us
  other arithmetic: 12.8 us -> 2.48 us
  waiting for transfers between devices: 47.3 us -> 55.9 us
  loops' own time: 7.89 us -> 0 us
  matrix products: 7.5 us -> 0 us
    gather x8 -> x0, local copies, waits for them, and re-layouts: 58.3 us -> none  [conv_block(): gathered = window[:, local_index] * present.astype(jnp.bfloat16)[None]]
    pallas_call x0 -> x1, Pallas kernels: none -> 11.2 us  [per_device(): pl.pallas_call(subtree_kernel, out_shape=(jax.ShapeDtypeStruct((all_merge...]
    another operation x1 -> x0, loops' own time: 7.89 us -> none  [tap_conv(): lax.map(conv_block, jnp.arange(pieces, dtype=jnp.int32) * block_rows)]
    dot_general x6 -> x0, matrix products: 7.5 us -> none  [the longest x4 6.47 us: conv_block(): jnp.einsum('ckr,kco->or', gathered, weight, preferred_element_type=jnp.fl...]
    reduce_scatter x1, waiting for transfers between devices: 13.3 us -> 19 us  [per_device(): lax.psum_scatter(weight_full, 'chan', scatter_dimension=2, tiled=True)]
    convert_element_type x8 -> x1, other arithmetic: 5.47 us -> 0.01 us  [per_device(): alive = living_rows.astype(jnp.float32)]
    all_to_all x1, waiting for transfers between devices: 0.01 us -> 2.99 us  [per_device(): lax.all_to_all(fetched, 'chan', split_axis=1, concat_axis=0, tiled=True)]
    concatenate x1, other arithmetic: 2.89 us -> 0.25 us  [per_device(): extended = jnp.concatenate([before, features, after], axis=1)]
  transfers between devices with their start and end apart: 7 -> 7, of which waited for: 2 -> 3; matrix products, arithmetic and copies ran while one was open for 48% -> 21% of each run, Pallas kernels for 0% -> 0%
where the time goes in v1:
time: 166 us; the launch traced here: 165 us
  waiting for transfers between devices  55.9 us (34%)
  local copies, waits for them, and re-layouts  35.5 us (21%)
  blocking collectives  24.8 us (15%)
  starting transfers between devices  20.1 us (12%)
  between operations  15 us (9%)
  Pallas kernels  11.2 us (7%)
  other arithmetic  2.48 us (1%)
    psum x1, waiting for transfers between devices, per_device(): lax.psum(weight_term, 'leaf') / math.sqrt(KIDS * group_count)  33.9 us
    scatter x2, local copies, waits for them, and re-layouts, per_device(): outbox = outbox.at[:, target_owner, within].set(merged, mode='drop')  26.1 us
    reduce_scatter x1, waiting for transfers between devices, per_device(): lax.psum_scatter(weight_full, 'chan', scatter_dimension=2, tiled=True)  19 us
    all_to_all x1, blocking collectives, per_device(): lax.all_to_all(outbox, 'leaf', split_axis=1, concat_axis=1, tiled=True)  12.3 us
    pallas_call x1, Pallas kernels, per_device(): pl.pallas_call(subtree_kernel, out_shape=(jax.ShapeDtypeStruct((all_merge...  11.2 us
    all_to_all x1, starting transfers between devices, per_device(): lax.all_to_all(parent_grad.reshape(out_merge, peer_count, pair_slots), 'l...  7.09 us
    all_gather x1, blocking collectives, per_device(): conv_all = lax.all_gather(conv_weight, 'chan', axis=2, tiled=True)  6.73 us
    ppermute x2, starting transfers between devices, passed_along(): lax.ppermute(value, axis, [(source, source + steps) for source in range(i...  6.17 us
  transfers between devices with their start and end apart: 7, of which 3 were waited for; matrix products, arithmetic and copies ran while one was open for 21% of the time, Pallas kernels for 0%

profile of v1, /device:TPU:0, one launch (start us, length us, event | category | flops | bytes accessed | tf_op | source)
XLA Modules:
  0.0 165.0 jit_solution(11804928164334978003)
XLA Ops:
  7.2 1.0 fusion.9
  8.2 4.9 %collective-permute-start = (bf16[64,1024]{1,0:T(8,128)(2,1)S(1)}, bf16[64,1024]{1,0:T(8,128)(2,1)S(1)}, u32[]{:S(2)}, u32[]{:S(2)}) collective-permute-start(bf16[64,1024]{1,0:T(8,128)(2,1)S(1)} %get-tuple-element.11), channel_id=1, source_target_pairs={{0,4},{4,8},{8,12},{12,16},{16,20},{20,24},{24,28},{1,5},{5,9},{9,... | collective-permute-start | bytes 393224 | tf_op jit(solution)/shard_map/ppermute | solution.py:58
  13.1 1.3 collective-permute-start.1
  14.6 0.7 reshape.80
  15.3 7.1 %all-to-all-start = ((bf16[8,2,1024]{2,1,0:T(2,128)(2,1)}), bf16[8,2,1024]{2,1,0:T(2,128)(2,1)S(1)}, u32[]{:S(2)}, u32[]{:S(2)}) async-start(bf16[8,2,1024]{2,1,0:T(2,128)(2,1)} %reshape.80), calls=%async_computation | async-start | bytes 65536 | tf_op jit(solution)/shard_map/all_to_all | solution.py:90
  23.1 6.7 %all_gather.6 = bf16[27,64,64]{1,2,0:T(8,128)(2,1)S(1)} all-gather(bf16[27,64,16]{1,2,0:T(8,128)(2,1)S(1)} %copy-done.2), channel_id=1, replica_groups=mesh['leaf'=8,'chan'=4] {'chan'}, dimensions={2}, use_global_device_ids=true | all-gather | bytes 276480 | tf_op jit(solution)/shard_map/all_gather | solution.py:79
  29.8 0.3 copy.36
  30.1 0.4 reshape.57
  30.6 0.4 copy-done.3
  31.0 5.9 %all_gather.7 = bf16[8,64,128]{1,0,2:T(8,128)(2,1)S(1)} all-gather(bf16[8,64,32]{1,0,2:T(8,128)(2,1)S(1)} %copy.37), channel_id=1, replica_groups=mesh['leaf'=8,'chan'=4] {'chan'}, dimensions={2}, use_global_device_ids=true | all-gather | bytes 163840 | tf_op jit(solution)/shard_map/all_gather | solution.py:80
  37.5 3.2 %gather_fusion = bf16[512,32]{1,0:T(8,128)(2,1)S(1)} fusion(bf16[32,8,64]{0,2,1:T(8,128)(2,1)S(1)} %copy.41, s32[512]{0:T(512)S(1)} %bitcast.40), kind=kCustom, calls=%fused_computation | custom fusion | bytes 69632 | tf_op jit(solution)/shard_map/gather | solution.py:97
  40.8 0.6 broadcast_multiply_fusion.1
  41.4 3.3 %all-to-all-start.1 = ((bf16[32,4,128]{2,0,1:T(8,128)(2,1)}), bf16[32,4,128]{2,0,1:T(8,128)(2,1)S(1)}, u32[]{:S(2)}, u32[]{:S(2)}) async-start(bf16[32,4,128]{2,0,1:T(8,128)(2,1)} %broadcast_multiply_fusion.1), calls=%async_computation.1 | async-start | bytes 65536 | tf_op jit(solution)/shard_map/all_to_all | solution.py:98
  45.2 0.3 reshape.55
  45.6 3.0 %all-to-all-done.1 = bf16[32,4,128]{2,0,1:T(8,128)(2,1)S(1)} async-done(((bf16[32,4,128]{2,0,1:T(8,128)(2,1)}), bf16[32,4,128]{2,0,1:T(8,128)(2,1)S(1)}, u32[]{:S(2)}, u32[]{:S(2)}) %all-to-all-start.1) | async-done | bytes 32800 | tf_op jit(solution)/shard_map/all_to_all | solution.py:98
  48.6 11.2 %shard_map.86 = (bf16[128,128]{1,0:T(8,128)(2,1)}, f32[512,128]{1,0:T(8,128)S(1)}) custom-call(bf16[768,256]{1,0:T(8,128)(2,1)S(1)} %bitcast.34, s32[27,1024]{1,0:T(8,128)S(1)} %constant_dynamic-slice_fusion.offsets, f32[1,1024]{1,0:T(1,128)S(1)} %compare_convert_fusion.alive, bf16[64,1728]{1,0:T(8,128)(2,1)S(1)} %bitcast.35, bf16[128,512]{1,0:T(8,128)(2,1)S(1)} %bitcast.36, ...), custom_call_target="tpu_custom_call" | custom-call | tf_op jit(solution)/shard_map/pallas_call | solution.py:102
  59.8 1.0 copy.46
  60.8 3.3 %all-to-all-start.2 = ((bf16[4,32,128]{2,1,0:T(8,128)(2,1)}), bf16[4,32,128]{2,1,0:T(8,128)(2,1)S(1)}, u32[]{:S(2)}, u32[]{:S(2)}) async-start(bf16[4,32,128]{2,1,0:T(8,128)(2,1)} %bitcast.16), calls=%async_computation.2 | async-start | bytes 65536 | tf_op jit(solution)/shard_map/all_to_all | solution.py:118
  64.2 19.0 %reduce-scatter.2.cloned.1.call-done = f32[8,64,32]{1,2,0:T(8,128)} async-done(((f32[8,64,128]{1,2,0:T(8,128)}), f32[8,64,32]{1,2,0:T(8,128)}) %reduce-scatter.2.cloned.1.call-update) | async-done | bytes 65552 | tf_op jit(solution)/shard_map/reduce_scatter | solution.py:124
  83.3 26.0 %scatter_fusion = bf16[32,8,64]{0,2,1:T(8,128)(2,1)S(1)} fusion(bf16[32,8,64]{0,2,1:T(8,128)(2,1)S(1)} %broadcast_in_dim.20, s32[512]{0:T(512)S(1)} %bitcast.39, bf16[512,32]{1,0:T(8,128)(2,1)S(1)} %bitcast.47), kind=kCustom, calls=%fused_computation.1 | custom fusion | bytes 102400 | tf_op jit(solution)/shard_map/scatter | solution.py:120
  109.5 12.3 %all_to_all.45 = bf16[8,2,1024]{2,1,0:T(2,128)(2,1)S(1)} all-to-all(bf16[8,2,1024]{2,1,0:T(2,128)(2,1)S(1)} %reshape.82), channel_id=1, replica_groups=mesh['leaf'=8,'chan'=4] {'leaf'}, dimensions={0} | all-to-all | bytes 65536 | tf_op jit(solution)/shard_map/all_to_all | solution.py:121
  121.9 0.7 reshape.60
  122.7 33.9 %all-reduce.2.cloned.1.call-done = f32[8,64,32]{1,2,0:T(8,128)} async-done(((f32[8,64,32]{1,2,0:T(8,128)}), f32[8,64,32]{1,2,0:T(8,128)}) %all-reduce.2.cloned.1.call-update) | async-done | bytes 65552 | tf_op jit(solution)/shard_map/psum | solution.py:125
  156.6 1.6 broadcast_multiply_fusion
  (40 shorter events, 2.1 us)
Async XLA Ops:
  7.2 30.0 %copy-start = (s32[27,4096]{1,0:T(8,128)S(1)}, s32[27,4096]{1,0:T(8,128)}, u32[]{:S(2)}) copy-start(s32[27,4096]{1,0:T(8,128)} %param.8) | copy-start | bytes 1327108
  7.2 7.2 %copy-start.4 = (bf16[32,512]{1,0:T(8,128)(2,1)S(1)}, bf16[32,512]{1,0:T(8,128)(2,1)}, u32[]{:S(2)}) copy-start(bf16[32,512]{1,0:T(8,128)(2,1)} %param.13) | copy-start | bytes 98308
  8.2 36.7 %collective-permute-start = (bf16[64,1024]{1,0:T(8,128)(2,1)S(1)}, bf16[64,1024]{1,0:T(8,128)(2,1)S(1)}, u32[]{:S(2)}, u32[]{:S(2)}) collective-permute-start(bf16[64,1024]{1,0:T(8,128)(2,1)S(1)} %get-tuple-element.11), channel_id=1, source_target_pairs={{0,4},{4,8},{8,12},{12,16},{16,20},{20,24},{24,28},{1,5},{5,9},{9,... | collective-permute-start | bytes 393224 | tf_op jit(solution)/shard_map/ppermute | solution.py:58
  13.1 31.8 %collective-permute-start.1 = (bf16[64,1024]{1,0:T(8,128)(2,1)S(1)}, bf16[64,1024]{1,0:T(8,128)(2,1)S(1)}, u32[]{:S(2)}, u32[]{:S(2)}) collective-permute-start(bf16[64,1024]{1,0:T(8,128)(2,1)S(1)} %get-tuple-element.10), channel_id=1, source_target_pairs={{4,0},{8,4},{12,8},{16,12},{20,16},{24,20},{28,24},{5,1},{9,5},{13... | collective-permute-start | bytes 393224 | tf_op jit(solution)/shard_map/ppermute | solution.py:58
  14.6 8.5 %copy-start.2 = (bf16[27,64,16]{1,2,0:T(8,128)(2,1)S(1)}, bf16[27,64,16]{1,2,0:T(8,128)(2,1)}, u32[]{:S(2)}) copy-start(bf16[27,64,16]{1,2,0:T(8,128)(2,1)} %param.11) | copy-start | bytes 165892
  15.3 7.1 %copy-start.5 = (s32[512]{0:T(512)S(1)}, s32[512]{0:T(512)}, u32[]{:S(2)}) copy-start(s32[512]{0:T(512)} %param.10) | copy-start | bytes 6148
  15.3 22.0 %all-to-all-start = ((bf16[8,2,1024]{2,1,0:T(2,128)(2,1)}), bf16[8,2,1024]{2,1,0:T(2,128)(2,1)S(1)}, u32[]{:S(2)}, u32[]{:S(2)}) async-start(bf16[8,2,1024]{2,1,0:T(2,128)(2,1)} %reshape.80), calls=%async_computation | async-start | bytes 65536 | tf_op jit(solution)/shard_map/all_to_all | solution.py:90
  30.1 0.8 copy-start.3
  37.4 7.6 %copy-start.1 = (bf16[64,4096]{1,0:T(8,128)(2,1)S(1)}, bf16[64,4096]{1,0:T(8,128)(2,1)}, u32[]{:S(2)}) copy-start(bf16[64,4096]{1,0:T(8,128)(2,1)} %param.7) | copy-start | bytes 1572868
  41.4 7.2 %all-to-all-start.1 = ((bf16[32,4,128]{2,0,1:T(8,128)(2,1)}), bf16[32,4,128]{2,0,1:T(8,128)(2,1)S(1)}, u32[]{:S(2)}, u32[]{:S(2)}) async-start(bf16[32,4,128]{2,0,1:T(8,128)(2,1)} %broadcast_multiply_fusion.1), calls=%async_computation.1 | async-start | bytes 65536 | tf_op jit(solution)/shard_map/all_to_all | solution.py:98
  44.7 38.4 %reduce-scatter.2.cloned.1.call-start = ((), (), s32[]{:S(2)}) async-start(), calls=%async_computation.5 | async-start | bytes 655360 | tf_op jit(solution)/shard_map/reduce_scatter | solution.py:124
  60.8 22.3 %all-to-all-start.2 = ((bf16[4,32,128]{2,1,0:T(8,128)(2,1)}), bf16[4,32,128]{2,1,0:T(8,128)(2,1)S(1)}, u32[]{:S(2)}, u32[]{:S(2)}) async-start(bf16[4,32,128]{2,1,0:T(8,128)(2,1)} %bitcast.16), calls=%async_computation.2 | async-start | bytes 65536 | tf_op jit(solution)/shard_map/all_to_all | solution.py:118
  64.1 92.5 %all-reduce.2.cloned.1.call-start = ((), (), s32[]{:S(2)}) async-start(), calls=%async_computation.6 | async-start | bytes 262144 | tf_op jit(solution)/shard_map/psum | solution.py:125
Sparse Core Ops, SparseCore 0:
  60.9 22.1 reduce-scatter.1
  86.8 69.6 all-reduce.1

commit v2 on v1

v2 whole, which is shorter than its diff:
```python
import functools
import math

import jax
import jax.numpy as jnp
from jax import lax
from jax.experimental import pallas as pl
from jax.experimental.pallas import tpu as pltpu
from jax.sharding import PartitionSpec as P

KIDS = 8
HALO = 1024
LO = 256
BLOCK = 256
REACH = (2 * HALO + BLOCK) // LO
LANES = 128
PIECE_ROWS = 16
MESH = pl.DeviceIdType.MESH


def each(count, step):
    if count <= 8:
        for turn in range(count):
            step(turn)
    else:
        lax.fori_loop(0, count, lambda turn, _: (step(turn), 0)[1], 0)


def octree_kernel(
    chans,
    leaves,
    features,
    neighbours,
    child_count,
    dest,
    conv_own,
    merge_own,
    cotangent,
    parents,
    grad,
    window,
    offsets,
    conv,
    merge,
    backward,
    fetched_out,
    fetched,
    picked,
    hidden,
    stacked,
    merged_out,
    merged,
    outbox,
    inbox,
    part,
    part_in,
    piece,
    piece_in,
    total,
    local_sem,
    halo_send,
    halo_recv,
    conv_send,
    conv_recv,
    merge_send,
    merge_recv,
    back_send,
    back_recv,
    fetched_send,
    fetched_recv,
    merged_send,
    merged_recv,
    box_send,
    box_recv,
    part_send,
    part_recv,
    piece_send,
    piece_recv,
    total_send,
    total_recv,
):
    leaf = lax.axis_index("leaf")
    chan = lax.axis_index("chan")
    width, row_count = features.shape
    taps = neighbours.shape[0]
    quarter = row_count // chans
    groups = quarter // KIDS
    group_count = row_count // KIDS
    pair_slots = group_count // leaves
    out_own = merge_own.shape[0]
    pieces = piece.shape[0]
    first_row = pl.multiple_of(chan * quarter, LO)

    def chan_copy(src, dst, send, recv, turn):
        peer = lax.rem(chan + turn + 1, chans)
        return pltpu.make_async_remote_copy(
            src_ref=src(peer), dst_ref=dst.at[chan], send_sem=send.at[turn],
            recv_sem=recv.at[chan], device_id=(leaf, peer), device_id_type=MESH,
        )

    def chan_arrival(dst, send, recv, turn):
        peer = lax.rem(chan + turn + 1, chans)
        return pltpu.make_async_remote_copy(
            src_ref=dst.at[peer], dst_ref=dst.at[peer], send_sem=send.at[turn],
            recv_sem=recv.at[peer], device_id=(leaf, peer), device_id_type=MESH,
        )

    def leaf_copy(src, dst, send, recv, turn):
        peer = lax.rem(leaf + turn + 1, leaves)
        return pltpu.make_async_remote_copy(
            src_ref=src(peer), dst_ref=dst.at[leaf], send_sem=send.at[turn],
            recv_sem=recv.at[leaf], device_id=(peer, chan), device_id_type=MESH,
        )

    def leaf_arrival(dst, send, recv, turn):
        peer = lax.rem(leaf + turn + 1, leaves)
        return pltpu.make_async_remote_copy(
            src_ref=dst.at[peer], dst_ref=dst.at[peer], send_sem=send.at[turn],
            recv_sem=recv.at[peer], device_id=(peer, chan), device_id_type=MESH,
        )

    def near(at, size):
        return features.at[:, pl.ds(at, size)]

    left_local = pltpu.make_async_copy(
        near(pl.multiple_of(jnp.maximum(first_row - HALO, 0), LO), HALO),
        window.at[:, pl.ds(0, HALO)], local_sem.at[0],
    )
    right_local = pltpu.make_async_copy(
        near(pl.multiple_of(jnp.minimum(first_row + quarter, row_count - HALO), LO), HALO),
        window.at[:, pl.ds(HALO + quarter, HALO)], local_sem.at[1],
    )
    centre_local = pltpu.make_async_copy(
        near(first_row, quarter), window.at[:, pl.ds(HALO, quarter)], local_sem.at[2]
    )
    offsets_local = pltpu.make_async_copy(
        neighbours.at[:, pl.ds(first_row, quarter)], offsets, local_sem.at[3]
    )
    from_left = pltpu.make_async_remote_copy(
        src_ref=near(row_count - HALO, HALO), dst_ref=window.at[:, pl.ds(0, HALO)],
        send_sem=halo_send.at[0], recv_sem=halo_recv.at[0],
        device_id=(jnp.minimum(leaf + 1, leaves - 1), chan), device_id_type=MESH,
    )
    from_right = pltpu.make_async_remote_copy(
        src_ref=near(0, HALO), dst_ref=window.at[:, pl.ds(HALO + quarter, HALO)],
        send_sem=halo_send.at[1], recv_sem=halo_recv.at[1],
        device_id=(jnp.maximum(leaf - 1, 0), chan), device_id_type=MESH,
    )
    at_first = chan == 0
    at_last = chan == chans - 1

    offsets_local.start()
    centre_local.start()
    pl.when(jnp.logical_not(at_first))(left_local.start)
    pl.when(jnp.logical_not(at_last))(right_local.start)

    barrier = pltpu.get_barrier_semaphore()

    def greet_chan(turn):
        peer = lax.rem(chan + turn + 1, chans)
        pl.semaphore_signal(barrier, inc=1, device_id=(leaf, peer), device_id_type=MESH)

    def greet_leaf(turn):
        peer = lax.rem(leaf + turn + 1, leaves)
        pl.semaphore_signal(barrier, inc=1, device_id=(peer, chan), device_id_type=MESH)

    each(chans - 1, greet_chan)
    each(leaves - 1, greet_leaf)
    pl.semaphore_wait(barrier, chans + leaves - 2)

    pl.when(at_first & (leaf < leaves - 1))(from_left.start)
    pl.when(at_last & (leaf > 0))(from_right.start)
    sends = []

    def send_chan(src, dst, send, recv):
        each(chans - 1, lambda turn: chan_copy(src, dst, send, recv, turn).start())
        sends.append((chans - 1, lambda turn: chan_copy(src, dst, send, recv, turn).wait_send()))

    def send_leaf(src, dst, send, recv):
        each(leaves - 1, lambda turn: leaf_copy(src, dst, send, recv, turn).start())
        sends.append((leaves - 1, lambda turn: leaf_copy(src, dst, send, recv, turn).wait_send()))

    def take_chan(dst, send, recv):
        each(chans - 1, lambda turn: chan_arrival(dst, send, recv, turn).wait_recv())

    def take_leaf(dst, send, recv):
        each(leaves - 1, lambda turn: leaf_arrival(dst, send, recv, turn).wait_recv())

    send_chan(lambda peer: conv_own, conv, conv_send, conv_recv)
    send_leaf(lambda peer: cotangent.at[peer], backward, back_send, back_recv)
    send_chan(lambda peer: merge_own, merge, merge_send, merge_recv)
    conv[chan] = conv_own[...]
    merge[chan] = merge_own[...]
    backward[leaf] = cotangent[leaf]

    @pl.when(at_first & (leaf == 0))
    def _():
        window[:, :HALO] = jnp.zeros((width, HALO), jnp.bfloat16)

    @pl.when(at_last & (leaf == leaves - 1))
    def _():
        window[:, HALO + quarter :] = jnp.zeros((width, HALO), jnp.bfloat16)

    offsets_local.wait()
    centre_local.wait()
    pl.when(jnp.logical_not(at_first))(left_local.wait)
    pl.when(jnp.logical_not(at_last))(right_local.wait)
    pl.when(at_first & (leaf > 0))(from_left.wait_recv)
    pl.when(at_last & (leaf < leaves - 1))(from_right.wait_recv)

    slot = lax.broadcasted_iota(jnp.int32, (LO, BLOCK), 0).astype(jnp.float32).astype(jnp.bfloat16)
    local = lax.broadcasted_iota(jnp.int32, (1, BLOCK), 1)
    count = child_count[0]

    def pick(block):
        span = pl.ds(block * BLOCK, BLOCK)
        source = jnp.concatenate(
            [window[:, pl.ds((block + high) * LO, LO)] for high in range(REACH)], axis=0
        )

        def one(tap, _):
            offset = offsets[pl.ds(tap, 1), span]
            place = local + offset
            chunk = place // LO
            inner = jnp.where(offset >= 0, place - chunk * LO, -1)
            inner = inner.astype(jnp.float32).astype(jnp.bfloat16)
            hot = jnp.where(slot == inner, jnp.bfloat16(1), jnp.bfloat16(0))
            found = jnp.dot(source, hot, preferred_element_type=jnp.float32)
            taken = found[:width]
            for high in range(1, REACH):
                taken = jnp.where(chunk == high, found[high * width : (high + 1) * width], taken)
            picked[pl.ds(pl.multiple_of(tap * width, width), width), :] = taken.astype(jnp.bfloat16)
            return 0

        lax.fori_loop(0, taps, one, 0, unroll=9 if taps % 9 == 0 else 1)

    def convolve(block):
        span = pl.ds(block * BLOCK, BLOCK)
        weight = conv[...].reshape(width, taps * width)
        pre_act = jnp.dot(weight, picked[...], preferred_element_type=jnp.float32)
        living = first_row + block * BLOCK + local < count
        hidden[:, span] = jnp.where(living, jnp.maximum(pre_act, 0.0), 0.0).astype(jnp.bfloat16)

    pick(0)
    take_chan(conv, conv_send, conv_recv)
    convolve(0)

    take_leaf(backward, back_send, back_recv)
    owner = dest[...] // group_count
    for part_index in range(chans):
        mine = owner[part_index : part_index + 1]

        def gain(source, held):
            return jnp.where(mine == source, backward[source].astype(jnp.float32), held)

        nothing = jnp.zeros((out_own, groups), jnp.float32)
        held = lax.fori_loop(0, leaves, gain, nothing, unroll=8)
        fetched_out[part_index] = held.astype(jnp.bfloat16)
    send_chan(lambda peer: fetched_out.at[peer], fetched, fetched_send, fetched_recv)
    fetched[chan] = fetched_out[chan]

    for block in range(1, quarter // BLOCK):
        pick(block)
        convolve(block)

    source_row = lax.broadcasted_iota(jnp.int32, (quarter, groups), 0)
    group_row = lax.broadcasted_iota(jnp.int32, (quarter, groups), 1) * KIDS
    for kid in range(KIDS):
        order = jnp.where(source_row == group_row + kid, 1.0, 0.0).astype(jnp.bfloat16)
        sorted_kid = jnp.dot(hidden[...], order, preferred_element_type=jnp.float32)
        stacked[pl.ds(kid * width, width), :] = sorted_kid.astype(jnp.bfloat16)

    take_chan(fetched, fetched_send, fetched_recv)
    part[...] = lax.dot_general(
        fetched[...].reshape(chans * out_own, groups), stacked[...],
        (((1,), (1,)), ((), ())), preferred_element_type=jnp.float32,
    ).reshape(part.shape)
    send_chan(lambda peer: part.at[peer], part_in, part_send, part_recv)

    take_chan(merge, merge_send, merge_recv)
    merged_out[...] = jnp.dot(
        merge[...].reshape(chans * out_own, KIDS * width), stacked[...],
        preferred_element_type=jnp.float32,
    ).astype(jnp.bfloat16).reshape(merged_out.shape)
    send_chan(lambda peer: merged_out.at[peer], merged, merged_send, merged_recv)
    merged[chan] = merged_out[chan]

    part_in[chan] = part[chan]
    take_chan(part_in, part_send, part_recv)
    term = part_in[0]
    for source in range(1, chans):
        term = term + part_in[source]
    across = KIDS * width // LANES
    for index in range(pieces):
        row, lane = index // across * PIECE_ROWS, index % across * LANES
        piece[index] = term[row : row + PIECE_ROWS, lane : lane + LANES]

    def piece_copy(turn):
        target = lax.rem(leaf + turn, pieces)
        return target, pltpu.make_async_remote_copy(
            src_ref=piece.at[target], dst_ref=piece_in.at[leaf], send_sem=piece_send.at[turn],
            recv_sem=piece_recv.at[leaf], device_id=(target, chan), device_id_type=MESH,
        )

    for turn in range(pieces):
        target, copy = piece_copy(turn)
        pl.when(target != leaf)(copy.start)

    take_chan(merged, merged_send, merged_recv)

    def fill_all(target, _):
        held = jnp.zeros((out_own, groups), jnp.float32)
        for source in range(chans):
            mine = owner[source : source + 1]
            held = held + jnp.where(mine == target, merged[source].astype(jnp.float32), 0.0)
        outbox[target] = held.astype(jnp.bfloat16)
        return 0

    lax.fori_loop(0, leaves, fill_all, 0, unroll=8)
    send_leaf(lambda peer: outbox.at[peer], inbox, box_send, box_recv)
    inbox[leaf] = outbox[leaf]

    @pl.when(leaf < pieces)
    def _():
        piece_in[leaf] = piece[leaf]
        take_leaf(piece_in, piece_send, piece_recv)

        def add(source, held):
            return held + piece_in[source]

        held = lax.fori_loop(1, leaves, add, piece_in[0], unroll=7 if leaves == 8 else 1)
        total[leaf] = held * (1.0 / math.sqrt(KIDS * group_count))
        each(leaves - 1, lambda turn: leaf_copy(
            lambda peer: total.at[leaf], total, total_send, total_recv, turn).start())

    take_leaf(inbox, box_send, box_recv)
    lane = lax.broadcasted_iota(jnp.int32, (1, LANES), 1) // pair_slots
    per_tile = LANES // pair_slots
    for tile in range(leaves // per_tile):
        whole = jnp.zeros((out_own, LANES), jnp.float32)
        for inside in range(per_tile):
            folded = inbox[tile * per_tile + inside].astype(jnp.float32)
            shift = pair_slots
            while shift < LANES:
                folded = folded + pltpu.roll(folded, shift, 1)
                shift *= 2
            whole = jnp.where(lane == inside, folded, whole)
        parents[:, pl.ds(tile * LANES, LANES)] = whole.astype(jnp.bfloat16)

    for index in range(pieces):
        arrival = pltpu.make_async_remote_copy(
            src_ref=total.at[index], dst_ref=total.at[index], send_sem=total_send.at[0],
            recv_sem=total_recv.at[index], device_id=(index, chan), device_id_type=MESH,
        )
        pl.when(leaf != index)(arrival.wait_recv)
    for index in range(pieces):
        row, lane_at = index // across * PIECE_ROWS, index % across * LANES
        grad[row : row + PIECE_ROWS, lane_at : lane_at + LANES] = total[index]

    pl.when(at_first & (leaf < leaves - 1))(from_left.wait_send)
    pl.when(at_last & (leaf > 0))(from_right.wait_send)
    for number, wait in sends:
        each(number, wait)
    for turn in range(pieces):
        target, copy = piece_copy(turn)
        pl.when(target != leaf)(copy.wait_send)

    @pl.when(leaf < pieces)
    def _():
        each(leaves - 1, lambda turn: leaf_copy(
            lambda peer: total.at[leaf], total, total_send, total_recv, turn).wait_send())


def per_device(features, neighbours, child_count, dest, conv_weight, merge_weight, parent_grad):
    width, row_count = features.shape
    taps = neighbours.shape[0]
    out_own = merge_weight.shape[2]
    group_count = row_count // KIDS
    leaves = lax.axis_size("leaf")
    chans = lax.axis_size("chan")
    pair_slots = group_count // leaves
    quarter = row_count // chans
    groups = quarter // KIDS
    repeats = groups // pair_slots
    pieces = min(leaves, out_own * KIDS * width // (PIECE_ROWS * LANES))
    conv_own = conv_weight.reshape(taps * width, -1).T
    merge_own = merge_weight.reshape(KIDS * width, -1).T
    blocks = parent_grad.reshape(out_own, leaves, 1, pair_slots)
    cotangent = jnp.broadcast_to(blocks, (out_own, leaves, repeats, pair_slots))
    cotangent = cotangent.reshape(out_own, leaves, groups).swapaxes(0, 1)

    anywhere = pl.BlockSpec(memory_space=pl.ANY)
    whole = pl.BlockSpec(memory_space=pltpu.VMEM)
    scalars = pl.BlockSpec(memory_space=pltpu.SMEM)
    bf16, f32 = jnp.bfloat16, jnp.float32

    def sems(*counts):
        return [pltpu.SemaphoreType.DMA((count,)) for count in counts]

    parents, grad = pl.pallas_call(
        functools.partial(octree_kernel, chans, leaves),
        out_shape=(
            jax.ShapeDtypeStruct((out_own, group_count), bf16),
            jax.ShapeDtypeStruct((out_own, KIDS * width), f32),
        ),
        in_specs=[anywhere, anywhere, scalars] + [whole] * 4,
        out_specs=(whole, whole),
        scratch_shapes=[
            pltpu.VMEM((width, quarter + 2 * HALO), bf16),
            pltpu.VMEM((taps, quarter), jnp.int32),
            pltpu.VMEM((chans, width // chans, taps * width), bf16),
            pltpu.VMEM((chans, out_own, KIDS * width), bf16),
            pltpu.VMEM((leaves, out_own, groups), bf16),
            pltpu.VMEM((chans, out_own, groups), bf16),
            pltpu.VMEM((chans, out_own, groups), bf16),
            pltpu.VMEM((taps * width, BLOCK), bf16),
            pltpu.VMEM((width, quarter), bf16),
            pltpu.VMEM((KIDS * width, groups), bf16),
            pltpu.VMEM((chans, out_own, groups), bf16),
            pltpu.VMEM((chans, out_own, groups), bf16),
            pltpu.VMEM((leaves, out_own, groups), bf16),
            pltpu.VMEM((leaves, out_own, groups), bf16),
            pltpu.VMEM((chans, out_own, KIDS * width), f32),
            pltpu.VMEM((chans, out_own, KIDS * width), f32),
            pltpu.VMEM((pieces, PIECE_ROWS, LANES), f32),
            pltpu.VMEM((leaves, PIECE_ROWS, LANES), f32),
            pltpu.VMEM((pieces, PIECE_ROWS, LANES), f32),
        ]
        + sems(4, 2, 2)
        + sems(chans, chans, chans, chans)
        + sems(leaves, leaves)
        + sems(chans, chans, chans, chans)
        + sems(leaves, leaves)
        + sems(chans, chans)
        + sems(pieces, leaves)
        + sems(leaves, leaves),
        compiler_params=pltpu.CompilerParams(
            collective_id=0, has_side_effects=True, vmem_limit_bytes=40 * 1024 * 1024
        ),
    )(
        features,
        neighbours,
        child_count,
        dest.reshape(chans, groups),
        conv_own,
        merge_own,
        cotangent,
    )
    return (parents, grad.T.reshape(KIDS, width, out_own))


def solution(mesh):
    in_specs = (
        P(None, "leaf"),
        P(None, "leaf"),
        P("leaf"),
        P("leaf"),
        P(None, None, "chan"),
        P(None, None, "chan"),
        P("chan", "leaf"),
    )
    out_specs = (P("chan", "leaf"), P(None, None, "chan"))
    return jax.shard_map(
        per_device, mesh=mesh, in_specs=in_specs, out_specs=out_specs, check_vma=False
    )
```

time: 166 us -> 41.1 us (0.25)
  waiting for transfers between devices: 55.9 us -> 0 us
  local copies, waits for them, and re-layouts: 35.5 us -> 4.19 us
  blocking collectives: 24.8 us -> 0 us
  Pallas kernels: 11.2 us -> 35.3 us
  starting transfers between devices: 20.1 us -> 0 us
  between operations: 15 us -> 1.35 us
  other arithmetic: 2.48 us -> 0 us
    psum x1 -> x0, waiting for transfers between devices: 33.9 us -> none  [per_device(): lax.psum(weight_term, 'leaf') / math.sqrt(KIDS * group_count)]
    scatter x2 -> x0, local copies, waits for them, and re-layouts: 26.1 us -> none  [per_device(): outbox = outbox.at[:, target_owner, within].set(merged, mode='drop')]
    pallas_call x1, Pallas kernels: 11.2 us -> 35.3 us  [per_device(): pl.pallas_call(functools.partial(octree_kernel, chans, leaves), out_shape...]
    reduce_scatter x1 -> x0, waiting for transfers between devices: 19 us -> none  [per_device(): lax.psum_scatter(weight_full, 'chan', scatter_dimension=2, tiled=True)]
    all_to_all x3 -> x0, starting transfers between devices: 13.6 us -> none  [the longest x1 7.09 us: per_device(): lax.all_to_all(parent_grad.reshape(out_merge, peer_count, pair_slots), 'l...]
    all_gather x2 -> x0, blocking collectives: 12.6 us -> none  [the longest x1 6.73 us: per_device(): conv_all = lax.all_gather(conv_weight, 'chan', axis=2, tiled=True)]
    all_to_all x1 -> x0, blocking collectives: 12.3 us -> none  [per_device(): lax.all_to_all(outbox, 'leaf', split_axis=1, concat_axis=1, tiled=True)]
    ppermute x2 -> x0, starting transfers between devices: 6.17 us -> none  [passed_along(): lax.ppermute(value, axis, [(source, source + steps) for source in range(i...]
  transfers between devices with their start and end apart: 7 -> 0, of which waited for: 3 -> 0; matrix products, arithmetic and copies ran while one was open for 21% -> 0% of each run, Pallas kernels for 0% -> 0%
where the time goes in v2:
time: 41.1 us; the launch traced here: 40.8 us
  Pallas kernels  35.3 us (86%)
  local copies, waits for them, and re-layouts  4.19 us (10%)
  between operations  1.35 us (3%)
    pallas_call x1, Pallas kernels, per_device(): pl.pallas_call(functools.partial(octree_kernel, chans, leaves), out_shape...  35.3 us
    unnamed x14, local copies, waits for them, and re-layouts  3.52 us

profile of v2, /device:TPU:0, one launch (start us, length us, event | category | flops | bytes accessed | tf_op | source)
XLA Modules:
  0.0 40.8 jit_solution(9404407004332551662)
XLA Ops:
  1.3 0.0 copy-start.3
  1.3 0.9 %copy.14 = bf16[8,64,32]{1,0,2:T(8,128)(2,1)S(1)} copy(bf16[8,64,32]{1,2,0:T(8,128)(2,1)} %param.12) | data formatting | bytes 65536 | tf_op args[5]
  2.2 0.0 copy-start.4
  2.2 0.1 reshape.23
  2.3 0.6 %copy-done.4 = bf16[32,512]{1,0:T(8,128)(2,1)S(1)} copy-done((bf16[32,512]{1,0:T(8,128)(2,1)S(1)}, bf16[32,512]{1,0:T(8,128)(2,1)}, u32[]{:S(2)}) %copy-start.4) | copy-done | bytes 32792
  3.0 0.0 copy-start
  3.0 0.0 copy-start.1
  3.0 0.1 broadcast_in_dim.7
  3.1 0.1 broadcast_in_dim.8
  3.2 0.1 reshape.24
  3.3 0.0 copy-done.3
  3.3 0.0 copy-start.2
  3.4 0.2 reshape.22
  3.5 0.5 %copy-done = bf16[64,4096]{1,0:T(8,128)(2,1)S(1)} copy-done((bf16[64,4096]{1,0:T(8,128)(2,1)S(1)}, bf16[64,4096]{1,0:T(8,128)(2,1)}, u32[]{:S(2)}) %copy-start) | copy-done | bytes 524312
  4.0 0.2 copy-done.1
  4.2 0.0 copy-done.2
  4.2 35.3 %shard_map.86 = (bf16[32,512]{1,0:T(8,128)(2,1)S(1)}, f32[32,512]{1,0:T(8,128)S(1)}) custom-call(bf16[64,4096]{1,0:T(8,128)(2,1)S(1)} %copy-done, s32[27,4096]{1,0:T(8,128)S(1)} %copy-done.1, s32[1]{0:T(128)S(6)} %copy.18.child_count, s32[4,128]{1,0:T(4,128)S(1)} %bitcast.17, bf16[16,1728]{1,0:T(8,128)(2,1)S(1)} %bitcast.14, bf16[32,512]{1,0:T(8,128)(2,1)S(1)} %bitcast.15, ...), custom_call_target="tpu_custom_call" | custom-call | tf_op jit(solution)/shard_map/pallas_call | solution.py:400
  39.4 0.1 reshape.25
  39.5 0.7 %copy.16 = f32[8,64,32]{1,2,0:T(8,128)} copy(f32[8,64,32]{1,0,2:T(8,128)S(1)} %reshape.25) | data formatting | bytes 131072
  40.2 0.6 %copy.19 = bf16[32,512]{1,0:T(8,128)(2,1)} copy(bf16[32,512]{1,0:T(8,128)(2,1)S(1)} %get-tuple-element.12) | data formatting | bytes 65536
  (2 shorter events, 0.0 us)
Async XLA Ops:
  1.3 2.0 %copy-start.3 = (bf16[27,64,16]{1,2,0:T(8,128)(2,1)S(1)}, bf16[27,64,16]{1,2,0:T(8,128)(2,1)}, u32[]{:S(2)}) copy-start(bf16[27,64,16]{1,2,0:T(8,128)(2,1)} %param.11) | copy-start | bytes 165892
  2.2 0.8 %copy-start.4 = (bf16[32,512]{1,0:T(8,128)(2,1)S(1)}, bf16[32,512]{1,0:T(8,128)(2,1)}, u32[]{:S(2)}) copy-start(bf16[32,512]{1,0:T(8,128)(2,1)} %param.13) | copy-start | bytes 98308
  3.0 1.0 %copy-start = (bf16[64,4096]{1,0:T(8,128)(2,1)S(1)}, bf16[64,4096]{1,0:T(8,128)(2,1)}, u32[]{:S(2)}) copy-start(bf16[64,4096]{1,0:T(8,128)(2,1)} %features.1) | copy-start | bytes 1572868
  3.0 1.2 %copy-start.1 = (s32[27,4096]{1,0:T(8,128)S(1)}, s32[27,4096]{1,0:T(8,128)}, u32[]{:S(2)}) copy-start(s32[27,4096]{1,0:T(8,128)} %neighbours.1) | copy-start | bytes 1327108
  3.3 0.8 %copy-start.2 = (s32[512]{0:T(512)S(1)}, s32[512]{0:T(512)}, u32[]{:S(2)}) copy-start(s32[512]{0:T(512)} %param.10) | copy-start | bytes 6148

commit v3 on v2

--- a/solution.py
+++ b/solution.py
@@ -35,24 +35,25 @@
     dest,
     conv_own,
     merge_own,
-    cotangent,
+    cotangent_own,
     parents,
     grad,
     window,
     offsets,
     conv,
     merge,
+    cotangent,
     backward,
     fetched_out,
     fetched,
     picked,
-    hidden,
     stacked,
     merged_out,
     merged,
     outbox,
     inbox,
     part,
+    part_out,
     part_in,
     piece,
     piece_in,
@@ -87,7 +88,7 @@
     groups = quarter // KIDS
     group_count = row_count // KIDS
     pair_slots = group_count // leaves
-    out_own = merge_own.shape[0]
+    out_own = merge_own.shape[1]
     pieces = piece.shape[0]
     first_row = pl.multiple_of(chan * quarter, LO)
 
@@ -166,6 +167,25 @@
 
     each(chans - 1, greet_chan)
     each(leaves - 1, greet_leaf)
+
+    for tap in range(0, taps, 2):
+        beside = jnp.concatenate([conv_own[at] for at in range(tap, min(tap + 2, taps))], axis=1)
+        conv[chan, :, tap * width : tap * width + beside.shape[1]] = beside
+    for kid in range(0, KIDS, 2):
+        beside = jnp.concatenate([merge_own[kid], merge_own[kid + 1]], axis=1)
+        merge[chan, :, kid * width : (kid + 2) * width] = beside
+    lane = lax.broadcasted_iota(jnp.int32, (1, LANES), 1) // pair_slots
+    per_tile = LANES // pair_slots
+    for tile in range(leaves // per_tile):
+        held = cotangent_own[:, tile * LANES : (tile + 1) * LANES].astype(jnp.float32)
+        for inside in range(per_tile):
+            spread = jnp.where(lane == inside, held, 0.0)
+            shift = pair_slots
+            while shift < LANES:
+                spread = spread + pltpu.roll(spread, shift, 1)
+                shift *= 2
+            cotangent[tile * per_tile + inside] = spread.astype(jnp.bfloat16)
+
     pl.semaphore_wait(barrier, chans + leaves - 2)
 
     pl.when(at_first & (leaf < leaves - 1))(from_left.start)
@@ -186,11 +206,9 @@
     def take_leaf(dst, send, recv):
         each(leaves - 1, lambda turn: leaf_arrival(dst, send, recv, turn).wait_recv())
 
-    send_chan(lambda peer: conv_own, conv, conv_send, conv_recv)
+    send_chan(lambda peer: conv.at[chan], conv, conv_send, conv_recv)
     send_leaf(lambda peer: cotangent.at[peer], backward, back_send, back_recv)
-    send_chan(lambda peer: merge_own, merge, merge_send, merge_recv)
-    conv[chan] = conv_own[...]
-    merge[chan] = merge_own[...]
+    send_chan(lambda peer: merge.at[chan], merge, merge_send, merge_recv)
     backward[leaf] = cotangent[leaf]
 
     @pl.when(at_first & (leaf == 0))
@@ -205,45 +223,101 @@
     centre_local.wait()
     pl.when(jnp.logical_not(at_first))(left_local.wait)
     pl.when(jnp.logical_not(at_last))(right_local.wait)
-    pl.when(at_first & (leaf > 0))(from_left.wait_recv)
-    pl.when(at_last & (leaf < leaves - 1))(from_right.wait_recv)
 
     slot = lax.broadcasted_iota(jnp.int32, (LO, BLOCK), 0).astype(jnp.float32).astype(jnp.bfloat16)
     local = lax.broadcasted_iota(jnp.int32, (1, BLOCK), 1)
     count = child_count[0]
 
+    blocks = quarter // BLOCK
+    flip = jnp.where(at_first, 1, 0)
+
+    def block_of(turn):
+        return jnp.where(at_first, blocks - 1 - turn, turn)
+
+    def span_of(block):
+        return pl.ds(pl.multiple_of(block * BLOCK, BLOCK), BLOCK)
+
+    def chunk_at(number):
+        return window[:, pl.ds(pl.multiple_of(number * LO, LO), LO)]
+
+    def over_taps(step):
+        lax.fori_loop(0, taps, lambda tap, _: (step(tap), 0)[1], 0, unroll=9 if taps % 9 == 0 else 1)
+
+    def split(tap, block):
+        offset = offsets[pl.ds(tap, 1), span_of(block)]
+        place = local + offset
+        chunk = place // LO
+        inner = jnp.where(offset >= 0, place - chunk * LO, -1)
+        inner = inner.astype(jnp.float32).astype(jnp.bfloat16)
+        return chunk, jnp.where(slot == inner, jnp.bfloat16(1), jnp.bfloat16(0))
+
+    def tap_rows(tap):
+        return pl.ds(pl.multiple_of(tap * width, width), width)
+
     def pick(block):
-        span = pl.ds(block * BLOCK, BLOCK)
-        source = jnp.concatenate(
-            [window[:, pl.ds((block + high) * LO, LO)] for high in range(REACH)], axis=0
-        )
-
-        def one(tap, _):
-            offset = offsets[pl.ds(tap, 1), span]
-            place = local + offset
-            chunk = place // LO
-            inner = jnp.where(offset >= 0, place - chunk * LO, -1)
-            inner = inner.astype(jnp.float32).astype(jnp.bfloat16)
-            hot = jnp.where(slot == inner, jnp.bfloat16(1), jnp.bfloat16(0))
+        source = jnp.concatenate([chunk_at(block + high) for high in range(REACH)], axis=0)
+
+        def one(tap):
+            chunk, hot = split(tap, block)
             found = jnp.dot(source, hot, preferred_element_type=jnp.float32)
             taken = found[:width]
             for high in range(1, REACH):
                 taken = jnp.where(chunk == high, found[high * width : (high + 1) * width], taken)
-            picked[pl.ds(pl.multiple_of(tap * width, width), width), :] = taken.astype(jnp.bfloat16)
-            return 0
-
-        lax.fori_loop(0, taps, one, 0, unroll=9 if taps % 9 == 0 else 1)
-
-    def convolve(block):
-        span = pl.ds(block * BLOCK, BLOCK)
+            picked[tap_rows(tap), :] = taken.astype(jnp.bfloat16)
+
+        over_taps(one)
+
+    def pick_local(block):
+        first = block + flip
+        source = jnp.concatenate([chunk_at(first + high) for high in range(REACH - 1)], axis=0)
+
+        def one(tap):
+            chunk, hot = split(tap, block)
+            found = jnp.dot(source, hot, preferred_element_type=jnp.float32)
+            taken = jnp.zeros((width, BLOCK), jnp.float32)
+            for high in range(REACH - 1):
+                here = chunk == high + flip
+                taken = jnp.where(here, found[high * width : (high + 1) * width], taken)
+            picked[tap_rows(tap), :] = taken.astype(jnp.bfloat16)
+
+        over_taps(one)
+
+    def pick_halo(block):
+        far = (REACH - 1) * (1 - flip)
+        source = chunk_at(block + far)
+
+        def one(tap):
+            chunk, hot = split(tap, block)
+            found = jnp.dot(source, hot, preferred_element_type=jnp.float32)
+            held = picked[tap_rows(tap), :].astype(jnp.float32)
+            picked[tap_rows(tap), :] = jnp.where(chunk == far, found, held).astype(jnp.bfloat16)
+
+        over_taps(one)
+
+    def convolve(block, fresh):
         weight = conv[...].reshape(width, taps * width)
         pre_act = jnp.dot(weight, picked[...], preferred_element_type=jnp.float32)
         living = first_row + block * BLOCK + local < count
-        hidden[:, span] = jnp.where(living, jnp.maximum(pre_act, 0.0), 0.0).astype(jnp.bfloat16)
-
-    pick(0)
+        hidden = jnp.where(living, jnp.maximum(pre_act, 0.0), 0.0).astype(jnp.bfloat16)
+        kids = BLOCK // groups
+        for kid in range(0, KIDS, kids):
+            wanted = lax.broadcasted_iota(jnp.int32, (1, BLOCK), 1)
+            wanted = wanted % groups * KIDS + kid + wanted // groups - block * BLOCK
+            wanted = jnp.where((wanted >= 0) & (wanted < BLOCK), wanted, -1)
+            wanted = wanted.astype(jnp.float32).astype(jnp.bfloat16)
+            order = jnp.where(slot == wanted, jnp.bfloat16(1), jnp.bfloat16(0))
+            moved = jnp.dot(hidden, order, preferred_element_type=jnp.float32).astype(jnp.bfloat16)
+            for inside in range(kids):
+                rows = pl.ds((kid + inside) * width, width)
+                new = moved[:, inside * groups : (inside + 1) * groups]
+                stacked[rows, :] = new if fresh else stacked[rows, :] + new
+
+    pick_local(block_of(0))
+    pl.when(at_first & (leaf > 0))(from_left.wait_recv)
+    pl.when(at_last & (leaf < leaves - 1))(from_right.wait_recv)
+    pick_halo(block_of(0))
     take_chan(conv, conv_send, conv_recv)
-    convolve(0)
+    convolve(block_of(0), True)
 
     take_leaf(backward, back_send, back_recv)
     owner = dest[...] // group_count
@@ -259,23 +333,17 @@
     send_chan(lambda peer: fetched_out.at[peer], fetched, fetched_send, fetched_recv)
     fetched[chan] = fetched_out[chan]
 
-    for block in range(1, quarter // BLOCK):
-        pick(block)
-        convolve(block)
-
-    source_row = lax.broadcasted_iota(jnp.int32, (quarter, groups), 0)
-    group_row = lax.broadcasted_iota(jnp.int32, (quarter, groups), 1) * KIDS
-    for kid in range(KIDS):
-        order = jnp.where(source_row == group_row + kid, 1.0, 0.0).astype(jnp.bfloat16)
-        sorted_kid = jnp.dot(hidden[...], order, preferred_element_type=jnp.float32)
-        stacked[pl.ds(kid * width, width), :] = sorted_kid.astype(jnp.bfloat16)
+    for turn in range(1, blocks):
+        pick(block_of(turn))
+        convolve(block_of(turn), False)
 
     take_chan(fetched, fetched_send, fetched_recv)
     part[...] = lax.dot_general(
         fetched[...].reshape(chans * out_own, groups), stacked[...],
         (((1,), (1,)), ((), ())), preferred_element_type=jnp.float32,
     ).reshape(part.shape)
-    send_chan(lambda peer: part.at[peer], part_in, part_send, part_recv)
+    part_out[...] = part[...].astype(jnp.bfloat16)
+    send_chan(lambda peer: part_out.at[peer], part_in, part_send, part_recv)
 
     take_chan(merge, merge_send, merge_recv)
     merged_out[...] = jnp.dot(
@@ -285,15 +353,14 @@
     send_chan(lambda peer: merged_out.at[peer], merged, merged_send, merged_recv)
     merged[chan] = merged_out[chan]
 
-    part_in[chan] = part[chan]
     take_chan(part_in, part_send, part_recv)
-    term = part_in[0]
-    for source in range(1, chans):
-        term = term + part_in[source]
+    term = part[chan]
+    for turn in range(1, chans):
+        term = term + part_in[lax.rem(chan + turn, chans)].astype(jnp.float32)
     across = KIDS * width // LANES
     for index in range(pieces):
-        row, lane = index // across * PIECE_ROWS, index % across * LANES
-        piece[index] = term[row : row + PIECE_ROWS, lane : lane + LANES]
+        row, column = index // across * PIECE_ROWS, index % across * LANES
+        piece[index] = term[row : row + PIECE_ROWS, column : column + LANES]
 
     def piece_copy(turn):
         target = lax.rem(leaf + turn, pieces)
@@ -334,8 +401,6 @@
             lambda peer: total.at[leaf], total, total_send, total_recv, turn).start())
 
     take_leaf(inbox, box_send, box_recv)
-    lane = lax.broadcasted_iota(jnp.int32, (1, LANES), 1) // pair_slots
-    per_tile = LANES // pair_slots
     for tile in range(leaves // per_tile):
         whole = jnp.zeros((out_own, LANES), jnp.float32)
         for inside in range(per_tile):
@@ -354,8 +419,11 @@
         )
         pl.when(leaf != index)(arrival.wait_recv)
     for index in range(pieces):
-        row, lane_at = index // across * PIECE_ROWS, index % across * LANES
-        grad[row : row + PIECE_ROWS, lane_at : lane_at + LANES] = total[index]
+        row, kid = index // across * PIECE_ROWS, index % across * (LANES // width)
+        summed = total[index]
+        for inside in range(LANES // width):
+            one_kid = summed[:, inside * width : (inside + 1) * width]
+            grad[kid + inside, row : row + PIECE_ROWS, :] = one_kid
 
     pl.when(at_first & (leaf < leaves - 1))(from_left.wait_send)
     pl.when(at_last & (leaf > 0))(from_right.wait_send)
@@ -378,17 +446,9 @@
     group_count = row_count // KIDS
     leaves = lax.axis_size("leaf")
     chans = lax.axis_size("chan")
-    pair_slots = group_count // leaves
     quarter = row_count // chans
     groups = quarter // KIDS
-    repeats = groups // pair_slots
     pieces = min(leaves, out_own * KIDS * width // (PIECE_ROWS * LANES))
-    conv_own = conv_weight.reshape(taps * width, -1).T
-    merge_own = merge_weight.reshape(KIDS * width, -1).T
-    blocks = parent_grad.reshape(out_own, leaves, 1, pair_slots)
-    cotangent = jnp.broadcast_to(blocks, (out_own, leaves, repeats, pair_slots))
-    cotangent = cotangent.reshape(out_own, leaves, groups).swapaxes(0, 1)
-
     anywhere = pl.BlockSpec(memory_space=pl.ANY)
     whole = pl.BlockSpec(memory_space=pltpu.VMEM)
     scalars = pl.BlockSpec(memory_space=pltpu.SMEM)
@@ -401,7 +461,7 @@
         functools.partial(octree_kernel, chans, leaves),
         out_shape=(
             jax.ShapeDtypeStruct((out_own, group_count), bf16),
-            jax.ShapeDtypeStruct((out_own, KIDS * width), f32),
+            jax.ShapeDtypeStruct((KIDS, out_own, width), f32),
         ),
         in_specs=[anywhere, anywhere, scalars] + [whole] * 4,
         out_specs=(whole, whole),
@@ -411,17 +471,18 @@
             pltpu.VMEM((chans, width // chans, taps * width), bf16),
             pltpu.VMEM((chans, out_own, KIDS * width), bf16),
             pltpu.VMEM((leaves, out_own, groups), bf16),
+            pltpu.VMEM((leaves, out_own, groups), bf16),
             pltpu.VMEM((chans, out_own, groups), bf16),
             pltpu.VMEM((chans, out_own, groups), bf16),
             pltpu.VMEM((taps * width, BLOCK), bf16),
-            pltpu.VMEM((width, quarter), bf16),
             pltpu.VMEM((KIDS * width, groups), bf16),
             pltpu.VMEM((chans, out_own, groups), bf16),
             pltpu.VMEM((chans, out_own, groups), bf16),
             pltpu.VMEM((leaves, out_own, groups), bf16),
             pltpu.VMEM((leaves, out_own, groups), bf16),
             pltpu.VMEM((chans, out_own, KIDS * width), f32),
-            pltpu.VMEM((chans, out_own, KIDS * width), f32),
+            pltpu.VMEM((chans, out_own, KIDS * width), bf16),
+            pltpu.VMEM((chans, out_own, KIDS * width), bf16),
             pltpu.VMEM((pieces, PIECE_ROWS, LANES), f32),
             pltpu.VMEM((leaves, PIECE_ROWS, LANES), f32),
             pltpu.VMEM((pieces, PIECE_ROWS, LANES), f32),
@@ -435,18 +496,18 @@
         + sems(pieces, leaves)
         + sems(leaves, leaves),
         compiler_params=pltpu.CompilerParams(
-            collective_id=0, has_side_effects=True, vmem_limit_bytes=40 * 1024 * 1024
+            collective_id=0, has_side_effects=True, vmem_limit_bytes=56 * 1024 * 1024
         ),
     )(
         features,
         neighbours,
         child_count,
         dest.reshape(chans, groups),
-        conv_own,
-        merge_own,
-        cotangent,
-    )
-    return (parents, grad.T.reshape(KIDS, width, out_own))
+        conv_weight.swapaxes(1, 2),
+        merge_weight.swapaxes(1, 2),
+        parent_grad,
+    )
+    return (parents, grad.swapaxes(1, 2))
 
 
 def solution(mesh):

time: 41.1 us -> 40.4 us (0.983)
  local copies, waits for them, and re-layouts: 4.19 us -> 2.94 us
  Pallas kernels: 35.3 us -> 35.9 us
    pallas_call x1, Pallas kernels: 35.3 us -> 35.9 us  [per_device(): pl.pallas_call(functools.partial(octree_kernel, chans, leaves), out_shape...]
    unnamed x14 -> x2, local copies, waits for them, and re-layouts: 3.52 us -> 2.94 us
    reshape x4 -> x0, local copies, waits for them, and re-layouts: 0.48 us -> none  [the longest x1 0.16 us: per_device(): conv_own = conv_weight.reshape(taps * width, -1).T]
where the time goes in v3:
time: 40.4 us; the launch traced here: 40.1 us
  Pallas kernels  35.9 us (89%)
  local copies, waits for them, and re-layouts  2.94 us (7%)
  between operations  1.29 us (3%)
    pallas_call x1, Pallas kernels, per_device(): pl.pallas_call(functools.partial(octree_kernel, chans, leaves), out_shape...  35.9 us
    unnamed x2, local copies, waits for them, and re-layouts  2.94 us

profile of v3, /device:TPU:0, one launch (start us, length us, event | category | flops | bytes accessed | tf_op | source)
XLA Modules:
  0.0 40.1 jit_solution(2964323054308412127)
XLA Ops:
  1.3 35.9 %shard_map.86 = (bf16[32,512]{1,0:T(8,128)(2,1)}, f32[8,32,64]{2,1,0:T(8,128)}) custom-call(bf16[64,4096]{1,0:T(8,128)(2,1)} %features.1, s32[27,4096]{1,0:T(8,128)} %neighbours.1, s32[1]{0:T(128)S(6)} %copy.11.child_count, s32[4,128]{1,0:T(4,128)} %bitcast.7, bf16[27,16,64]{2,1,0:T(8,128)(2,1)} %bitcast.5, bf16[8,32,64]{2,1,0:T(8,128)(2,1)} %bitcast.6, ...), custom_call_target="tpu_custom_call" | custom-call | tf_op jit(solution)/shard_map/pallas_call | solution.py:460
  37.2 1.4 %copy.12 = bf16[32,512]{1,0:T(8,128)(2,1)} copy(bf16[32,512]{1,0:T(8,128)(2,1)} %get-tuple-element.8) | data formatting | bytes 65536
  38.6 1.6 %copy.13 = f32[8,64,32]{1,2,0:T(8,128)} copy(f32[8,64,32]{1,2,0:T(8,128)} %bitcast.4) | data formatting | bytes 131072

commit v4 on v3

--- a/solution.py
+++ b/solution.py
@@ -229,6 +229,7 @@
     count = child_count[0]
 
     blocks = quarter // BLOCK
+    centre = taps // 2
     flip = jnp.where(at_first, 1, 0)
 
     def block_of(turn):
@@ -241,7 +242,8 @@
         return window[:, pl.ds(pl.multiple_of(number * LO, LO), LO)]
 
     def over_taps(step):
-        lax.fori_loop(0, taps, lambda tap, _: (step(tap), 0)[1], 0, unroll=9 if taps % 9 == 0 else 1)
+        for low, high in ((0, centre), (centre + 1, taps)):
+            lax.fori_loop(low, high, lambda tap, _: (step(tap), 0)[1], 0, unroll=high - low)
 
     def split(tap, block):
         offset = offsets[pl.ds(tap, 1), span_of(block)]
@@ -254,7 +256,11 @@
     def tap_rows(tap):
         return pl.ds(pl.multiple_of(tap * width, width), width)
 
+    def own_rows(block):
+        picked[pl.ds(centre * width, width), :] = chunk_at(block + HALO // LO)
+
     def pick(block):
+        own_rows(block)
         source = jnp.concatenate([chunk_at(block + high) for high in range(REACH)], axis=0)
 
         def one(tap):
@@ -269,6 +275,7 @@
 
     def pick_local(block):
         first = block + flip
+        own_rows(block)
         source = jnp.concatenate([chunk_at(first + high) for high in range(REACH - 1)], axis=0)
 
         def one(tap):
@@ -496,7 +503,7 @@
         + sems(pieces, leaves)
         + sems(leaves, leaves),
         compiler_params=pltpu.CompilerParams(
-            collective_id=0, has_side_effects=True, vmem_limit_bytes=56 * 1024 * 1024
+            collective_id=0, has_side_effects=True, vmem_limit_bytes=40 * 1024 * 1024
         ),
     )(
         features,

time: 40.4 us -> 40.3 us (level)
  Pallas kernels: 35.9 us -> 32.1 us
  local copies, waits for them, and re-layouts: 2.94 us -> 6.52 us
    pallas_call x1, Pallas kernels: 35.9 us -> 32.1 us  [per_device(): pl.pallas_call(functools.partial(octree_kernel, chans, leaves), out_shape...]
    unnamed x2 -> x14, local copies, waits for them, and re-layouts: 2.94 us -> 6.52 us
where the time goes in v4:
time: 40.3 us; the launch traced here: 40 us
  Pallas kernels  32.1 us (80%)
  local copies, waits for them, and re-layouts  6.52 us (16%)
  between operations  1.3 us (3%)
    pallas_call x1, Pallas kernels, per_device(): pl.pallas_call(functools.partial(octree_kernel, chans, leaves), out_shape...  32.1 us
    unnamed x14, local copies, waits for them, and re-layouts  6.52 us

profile of v4, /device:TPU:0, one launch (start us, length us, event | category | flops | bytes accessed | tf_op | source)
XLA Modules:
  0.0 40.0 jit_solution(1888193950821273765)
XLA Ops:
  1.3 0.0 copy-start.5
  1.3 0.7 %copy-done.5 = s32[512]{0:T(512)S(1)} copy-done((s32[512]{0:T(512)S(1)}, s32[512]{0:T(512)}, u32[]{:S(2)}) %copy-start.5) | copy-done | bytes 2072
  2.0 0.0 copy-start
  2.0 1.0 %copy-done = bf16[64,4096]{1,0:T(8,128)(2,1)S(1)} copy-done((bf16[64,4096]{1,0:T(8,128)(2,1)S(1)}, bf16[64,4096]{1,0:T(8,128)(2,1)}, u32[]{:S(2)}) %copy-start) | copy-done | bytes 524312
  3.0 0.0 copy-start.1
  3.0 1.0 %copy-done.1 = s32[27,4096]{1,0:T(8,128)S(1)} copy-done((s32[27,4096]{1,0:T(8,128)S(1)}, s32[27,4096]{1,0:T(8,128)}, u32[]{:S(2)}) %copy-start.1) | copy-done | bytes 442392
  4.0 0.0 copy-start.2
  4.0 0.9 %copy-done.2 = bf16[27,64,16]{1,2,0:T(8,128)(2,1)S(1)} copy-done((bf16[27,64,16]{1,2,0:T(8,128)(2,1)S(1)}, bf16[27,64,16]{1,2,0:T(8,128)(2,1)}, u32[]{:S(2)}) %copy-start.2) | copy-done | bytes 55320
  4.9 0.0 copy-start.3
  4.9 0.8 %copy-done.3 = bf16[8,64,32]{1,2,0:T(8,128)(2,1)S(1)} copy-done((bf16[8,64,32]{1,2,0:T(8,128)(2,1)S(1)}, bf16[8,64,32]{1,2,0:T(8,128)(2,1)}, u32[]{:S(2)}) %copy-start.3) | copy-done | bytes 32792
  5.8 0.0 copy-start.4
  5.8 0.8 %copy-done.4 = bf16[32,512]{1,0:T(8,128)(2,1)S(1)} copy-done((bf16[32,512]{1,0:T(8,128)(2,1)S(1)}, bf16[32,512]{1,0:T(8,128)(2,1)}, u32[]{:S(2)}) %copy-start.4) | copy-done | bytes 32792
  6.5 32.1 %shard_map.86 = (bf16[32,512]{1,0:T(8,128)(2,1)S(1)}, f32[8,32,64]{2,1,0:T(8,128)S(1)}) custom-call(bf16[64,4096]{1,0:T(8,128)(2,1)S(1)} %copy-done, s32[27,4096]{1,0:T(8,128)S(1)} %copy-done.1, s32[1]{0:T(128)S(6)} %copy.11.child_count, s32[4,128]{1,0:T(4,128)S(1)} %bitcast.7, bf16[27,16,64]{2,1,0:T(8,128)(2,1)S(1)} %bitcast.5, ...), custom_call_target="tpu_custom_call" | custom-call | tf_op jit(solution)/shard_map/pallas_call | solution.py:467
  38.7 0.6 %copy.12 = bf16[32,512]{1,0:T(8,128)(2,1)} copy(bf16[32,512]{1,0:T(8,128)(2,1)S(1)} %get-tuple-element.8) | data formatting | bytes 65536
  39.3 0.7 %copy.13 = f32[8,64,32]{1,2,0:T(8,128)} copy(f32[8,64,32]{1,2,0:T(8,128)S(1)} %bitcast.4) | data formatting | bytes 131072
Async XLA Ops:
  1.3 0.7 %copy-start.5 = (s32[512]{0:T(512)S(1)}, s32[512]{0:T(512)}, u32[]{:S(2)}) copy-start(s32[512]{0:T(512)} %param.10) | copy-start | bytes 6148
  2.0 1.0 %copy-start = (bf16[64,4096]{1,0:T(8,128)(2,1)S(1)}, bf16[64,4096]{1,0:T(8,128)(2,1)}, u32[]{:S(2)}) copy-start(bf16[64,4096]{1,0:T(8,128)(2,1)} %features.1) | copy-start | bytes 1572868
  3.0 1.0 %copy-start.1 = (s32[27,4096]{1,0:T(8,128)S(1)}, s32[27,4096]{1,0:T(8,128)}, u32[]{:S(2)}) copy-start(s32[27,4096]{1,0:T(8,128)} %neighbours.1) | copy-start | bytes 1327108
  4.0 0.9 %copy-start.2 = (bf16[27,64,16]{1,2,0:T(8,128)(2,1)S(1)}, bf16[27,64,16]{1,2,0:T(8,128)(2,1)}, u32[]{:S(2)}) copy-start(bf16[27,64,16]{1,2,0:T(8,128)(2,1)} %param.11) | copy-start | bytes 165892
  4.9 0.8 %copy-start.3 = (bf16[8,64,32]{1,2,0:T(8,128)(2,1)S(1)}, bf16[8,64,32]{1,2,0:T(8,128)(2,1)}, u32[]{:S(2)}) copy-start(bf16[8,64,32]{1,2,0:T(8,128)(2,1)} %param.12) | copy-start | bytes 98308
  5.8 0.8 %copy-start.4 = (bf16[32,512]{1,0:T(8,128)(2,1)S(1)}, bf16[32,512]{1,0:T(8,128)(2,1)}, u32[]{:S(2)}) copy-start(bf16[32,512]{1,0:T(8,128)(2,1)} %cotangent_own.1) | copy-start | bytes 98308

commit v5 on v4

--- a/solution.py
+++ b/solution.py
@@ -32,6 +32,12 @@
     features,
     neighbours,
     child_count,
+    dest_far,
+    conv_far,
+    merge_far,
+    cotangent_far,
+    parents_far,
+    grad_far,
     dest,
     conv_own,
     merge_own,
@@ -150,6 +156,14 @@
     at_first = chan == 0
     at_last = chan == chans - 1
 
+    owned = [
+        pltpu.make_async_copy(far, close, local_sem.at[4 + number])
+        for number, (far, close) in enumerate(
+            ((conv_far, conv_own), (cotangent_far, cotangent_own), (merge_far, merge_own), (dest_far, dest))
+        )
+    ]
+    for copy in owned:
+        copy.start()
     offsets_local.start()
     centre_local.start()
     pl.when(jnp.logical_not(at_first))(left_local.start)
@@ -168,6 +182,8 @@
     each(chans - 1, greet_chan)
     each(leaves - 1, greet_leaf)
 
+    for copy in owned:
+        copy.wait()
     for tap in range(0, taps, 2):
         beside = jnp.concatenate([conv_own[at] for at in range(tap, min(tap + 2, taps))], axis=1)
         conv[chan, :, tap * width : tap * width + beside.shape[1]] = beside
@@ -418,6 +434,8 @@
                 shift *= 2
             whole = jnp.where(lane == inside, folded, whole)
         parents[:, pl.ds(tile * LANES, LANES)] = whole.astype(jnp.bfloat16)
+    parents_done = pltpu.make_async_copy(parents, parents_far, local_sem.at[8])
+    parents_done.start()
 
     for index in range(pieces):
         arrival = pltpu.make_async_remote_copy(
@@ -431,6 +449,8 @@
         for inside in range(LANES // width):
             one_kid = summed[:, inside * width : (inside + 1) * width]
             grad[kid + inside, row : row + PIECE_ROWS, :] = one_kid
+    grad_done = pltpu.make_async_copy(grad, grad_far, local_sem.at[9])
+    grad_done.start()
 
     pl.when(at_first & (leaf < leaves - 1))(from_left.wait_send)
     pl.when(at_last & (leaf > 0))(from_right.wait_send)
@@ -444,6 +464,19 @@
     def _():
         each(leaves - 1, lambda turn: leaf_copy(
             lambda peer: total.at[leaf], total, total_send, total_recv, turn).wait_send())
+    parents_done.wait()
+    grad_done.wait()
+
+
+def settle_kernel(parents, grad, parents_out, grad_out, sem):
+    copies = (
+        pltpu.make_async_copy(parents, parents_out, sem.at[0]),
+        pltpu.make_async_copy(grad, grad_out, sem.at[1]),
+    )
+    for copy in copies:
+        copy.start()
+    for copy in copies:
+        copy.wait()
 
 
 def per_device(features, neighbours, child_count, dest, conv_weight, merge_weight, parent_grad):
@@ -457,7 +490,6 @@
     groups = quarter // KIDS
     pieces = min(leaves, out_own * KIDS * width // (PIECE_ROWS * LANES))
     anywhere = pl.BlockSpec(memory_space=pl.ANY)
-    whole = pl.BlockSpec(memory_space=pltpu.VMEM)
     scalars = pl.BlockSpec(memory_space=pltpu.SMEM)
     bf16, f32 = jnp.bfloat16, jnp.float32
 
@@ -470,9 +502,15 @@
             jax.ShapeDtypeStruct((out_own, group_count), bf16),
             jax.ShapeDtypeStruct((KIDS, out_own, width), f32),
         ),
-        in_specs=[anywhere, anywhere, scalars] + [whole] * 4,
-        out_specs=(whole, whole),
+        in_specs=[anywhere, anywhere, scalars] + [anywhere] * 4,
+        out_specs=(anywhere, anywhere),
         scratch_shapes=[
+            pltpu.VMEM((chans, groups), jnp.int32),
+            pltpu.VMEM((taps, width // chans, width), bf16),
+            pltpu.VMEM((KIDS, out_own, width), bf16),
+            pltpu.VMEM((out_own, group_count), bf16),
+            pltpu.VMEM((out_own, group_count), bf16),
+            pltpu.VMEM((KIDS, out_own, width), f32),
             pltpu.VMEM((width, quarter + 2 * HALO), bf16),
             pltpu.VMEM((taps, quarter), jnp.int32),
             pltpu.VMEM((chans, width // chans, taps * width), bf16),
@@ -494,7 +532,7 @@
             pltpu.VMEM((leaves, PIECE_ROWS, LANES), f32),
             pltpu.VMEM((pieces, PIECE_ROWS, LANES), f32),
         ]
-        + sems(4, 2, 2)
+        + sems(10, 2, 2)
         + sems(chans, chans, chans, chans)
         + sems(leaves, leaves)
         + sems(chans, chans, chans, chans)
@@ -503,7 +541,7 @@
         + sems(pieces, leaves)
         + sems(leaves, leaves),
         compiler_params=pltpu.CompilerParams(
-            collective_id=0, has_side_effects=True, vmem_limit_bytes=40 * 1024 * 1024
+            collective_id=0, has_side_effects=True, vmem_limit_bytes=56 * 1024 * 1024
         ),
     )(
         features,
@@ -514,6 +552,17 @@
         merge_weight.swapaxes(1, 2),
         parent_grad,
     )
+    parents, grad = pl.pallas_call(
+        settle_kernel,
+        out_shape=(
+            jax.ShapeDtypeStruct(parents.shape, bf16),
+            jax.ShapeDtypeStruct(grad.shape, f32),
+        ),
+        in_specs=[anywhere] * 2,
+        out_specs=(anywhere, anywhere),
+        scratch_shapes=sems(2),
+        compiler_params=pltpu.CompilerParams(vmem_limit_bytes=56 * 1024 * 1024),
+    )(parents, grad)
     return (parents, grad.swapaxes(1, 2))
 
 

time: 40.3 us -> 40 us (level)
  local copies, waits for them, and re-layouts: 6.52 us -> 0 us
  Pallas kernels: 32.1 us -> 38.6 us
    unnamed x14 -> x0, local copies, waits for them, and re-layouts: 6.52 us -> none
    pallas_call x0 -> x1, Pallas kernels: none -> 6.08 us  [per_device(): pl.pallas_call(settle_kernel, out_shape=(jax.ShapeDtypeStruct(parents.sha...]
where the time goes in v5:
time: 40 us; the launch traced here: 39.8 us
  Pallas kernels  38.6 us (96%)
  between operations  1.28 us (3%)
    pallas_call x1, Pallas kernels, per_device(): pl.pallas_call(functools.partial(octree_kernel, chans, leaves), out_shape...  32.5 us
    pallas_call x1, Pallas kernels, per_device(): pl.pallas_call(settle_kernel, out_shape=(jax.ShapeDtypeStruct(parents.sha...  6.08 us

profile of v5, /device:TPU:0, one launch (start us, length us, event | category | flops | bytes accessed | tf_op | source)
XLA Modules:
  0.0 39.8 jit_solution(3815321981538005799)
XLA Ops:
  1.3 32.5 %shard_map.86 = (bf16[32,512]{1,0:T(8,128)(2,1)}, f32[8,32,64]{2,1,0:T(8,128)}) custom-call(bf16[64,4096]{1,0:T(8,128)(2,1)} %features.1, s32[27,4096]{1,0:T(8,128)} %neighbours.1, s32[1]{0:T(128)S(6)} %copy.9.child_count, s32[4,128]{1,0:T(4,128)} %bitcast.6, bf16[27,16,64]{2,1,0:T(8,128)(2,1)} %bitcast.4, bf16[8,32,64]{2,1,0:T(8,128)(2,1)} %bitcast.5, ...), custom_call_target="tpu_custom_call" | custom-call | tf_op jit(solution)/shard_map/pallas_call | solution.py:499
  33.8 6.1 %shard_map.87 = (bf16[32,512]{1,0:T(8,128)(2,1)}, f32[8,32,64]{2,1,0:T(8,128)}) custom-call(bf16[32,512]{1,0:T(8,128)(2,1)} %get-tuple-element.6.parents, f32[8,32,64]{2,1,0:T(8,128)} %get-tuple-element.7.grad), custom_call_target="tpu_custom_call" | custom-call | tf_op jit(solution)/shard_map/pallas_call | solution.py:555
